TPU v7x, 32 devices: a whole 2x2x4 slice. The times are simulated.
32 devices in a mesh: members: 2 (over y), tiles: 4 (over z), rows: 2 (over x), lev: 2 (over core).
Axes of the slice: x: 2, y: 2, z: 4, core: 2. Of those that a mesh axis runs over, the one named last changes fastest.
Arguments:
- air_state: float32 [64, 48, 1536], P(('members', 'lev'), 'rows', 'tiles'), parts along dimension 0, may hold values from -6 to 6
- wind_east: float32 [64, 48, 1536], P(('members', 'lev'), 'rows', 'tiles'), parts along dimension 0, may hold values from -0.4 to 0.4
- wind_north: float32 [64, 48, 1536], P(('members', 'lev'), 'rows', 'tiles'), parts along dimension 0, may hold values from -0.4 to 0.4
- feedback_weight: float32 [32], P('lev'), may hold values from 0.2 to 1
- nest_west: int32 [4], P('members'), parts along dimension 0, may hold values from 1 to 1023
- nest_south: int32 [4], P('members'), parts along dimension 0, may hold values from 1 to 31
Outputs:
- new_state: float32 [64, 48, 1536], P(('members', 'lev'), 'rows', 'tiles'), parts along dimension 0
There are 2 independent parts, one for each index of `members`. A program takes and returns all parts, laid end to end along the dimension named above; an argument that names none is the same for every part. Nothing has to cross between parts.
Inputs may be any that keep to these rules, and one draw needn't show every extreme that they name: `nest_west`: the nest's footprint with one cell of margin lies inside the parent grid in both substeps.
All inputs are finite; a program needn't handle non-finite values.
Results may differ from a plain program's by a relative error of at most 0.000086.
Values sent between devices are 32-bit elements; how exact they have to be, the bound alone decides.
No kernel may reach another device: no remote copies, remote signals or barrier semaphores. Data moves between devices by JAX's collectives and lax.ppermute only.
A program may use at most 64 MiB of HBM per device.

v0:
```python
import functools
import math

import jax
import jax.numpy as jnp
import numpy as np
from jax import lax
from jax.experimental import pallas as pl
from jax.experimental.pallas import tpu as pltpu
from jax.sharding import PartitionSpec as P

VERTICAL_MIX = 0.1
PARENT_MIXING = 0.04
NEST_MIXING = 0.18
NEST_ADVECT = 1.5
NUDGING = 0.2


def padded_2(array, sides, width):
    for axis, dim in sides:
        size, length = (lax.axis_size(axis), array.shape[dim])
        up = [(i, (i + 1) % size) for i in range(size - 1)]
        down = [(j, i) for i, j in up]
        last = lax.slice_in_dim(array, length - width, length, axis=dim)
        first = lax.slice_in_dim(array, 0, width, axis=dim)
        before = lax.ppermute(last, axis, up)
        after = lax.ppermute(first, axis, down)
        array = jnp.concatenate([before, array, after], axis=dim)
    return array


def interp_table(cells):
    extended = jnp.arange(cells + 2, dtype=jnp.int32) - 1
    coarse = jnp.floor_divide(extended, 3)
    offset = extended - 3 * coarse
    fraction = jnp.abs(offset - 1).astype(jnp.float32) / 3.0
    nearest = coarse + 1
    beside = nearest + (offset - 1)
    slots = jnp.arange(cells // 3 + 2, dtype=jnp.int32)[:, None]
    first_part = jnp.where(
        slots == nearest[None, :], 1.0 - fraction[None, :], jnp.zeros((), jnp.float32)
    )
    second_part = jnp.where(slots == beside[None, :], fraction[None, :], jnp.zeros((), jnp.float32))
    return first_part + second_part


def tendency(padded, speed_east, speed_north, advect_scale, mixing_scale):
    centre = padded[1:-1, 1:-1, 1:-1]
    eastern = padded[1:-1, 1:-1, 2:]
    western = padded[1:-1, 1:-1, :-2]
    southern = padded[1:-1, 2:, 1:-1]
    northern = padded[1:-1, :-2, 1:-1]
    upper = padded[2:, 1:-1, 1:-1]
    lower = padded[:-2, 1:-1, 1:-1]
    advect = speed_east * (eastern - western) + speed_north * (southern - northern)
    horizontal = eastern + western + southern + northern - 4.0 * centre
    vertical = upper + lower - 2.0 * centre
    return -0.5 * advect_scale * advect + mixing_scale * horizontal + VERTICAL_MIX * vertical


def padded_block(block_field):
    return padded_2(block_field, (("tiles", 2), ("rows", 1), ("lev", 0)), 1)


def per_device(air_state, wind_east, wind_north, feedback_weight, nest_west, nest_south):
    levels, height, breadth = air_state.shape
    tile_count = lax.axis_size("tiles")
    row_count = lax.axis_size("rows")
    tile_index = lax.axis_index("tiles")
    row_index = lax.axis_index("rows")
    parent_tiles = 3 * tile_count // 4
    nest_tiles = tile_count - parent_tiles
    in_nest = tile_index >= parent_tiles
    nest_tile = tile_index - parent_tiles
    cross_x = breadth // 3 + 2
    cross_y = height // 3 + 2
    third_x = breadth // 3
    third_y = height // 3
    first_x = tile_index * breadth
    first_y = row_index * height
    columns = jnp.arange(breadth, dtype=jnp.int32)
    lines = jnp.arange(height, dtype=jnp.int32)
    targets_x = jnp.arange(tile_count, dtype=jnp.int32)
    targets_y = jnp.arange(row_count, dtype=jnp.int32)
    highest = lax.Precision.HIGHEST
    table_x = interp_table(breadth)
    table_y = interp_table(height)
    zero_value = jnp.zeros((), jnp.float32)

    def boundary(source, substep):
        anchor_x = nest_west[substep] + (targets_x - parent_tiles) * third_x - 1
        slot_x = jnp.arange(cross_x, dtype=jnp.int32)
        pick_x = (
            (first_x + columns)[None, :, None] == anchor_x[:, None, None] + slot_x[None, None, :]
        ) & (targets_x >= parent_tiles)[:, None, None]
        pick_x = pick_x.astype(jnp.float32)
        anchor_y = nest_south[substep] + targets_y * third_y - 1
        slot_y = jnp.arange(cross_y, dtype=jnp.int32)
        pick_y = (
            (first_y + lines)[None, :, None] == anchor_y[:, None, None] + slot_y[None, None, :]
        ).astype(jnp.float32)
        pieces = jnp.einsum("lyi,tij->tlyj", source, pick_x, precision=highest)
        merged = lax.all_to_all(pieces, "tiles", split_axis=0, concat_axis=0, tiled=True).sum(
            axis=0
        )
        pieces = jnp.einsum("lyj,ryw->rlwj", merged, pick_y, precision=highest)
        window = lax.all_to_all(pieces, "rows", split_axis=0, concat_axis=0, tiled=True).sum(axis=0)
        along = jnp.einsum("lwj,je->lwe", window, table_x, precision=highest)
        return jnp.einsum("lwe,wf->lfe", along, table_y, precision=highest)

    def assemble(block_field, fine):
        padded = padded_block(block_field)
        fine_padded = jnp.pad(fine, ((1, 1), (0, 0), (0, 0)))
        column_place = lax.broadcasted_iota(jnp.int32, padded.shape, 2)
        line_place = lax.broadcasted_iota(jnp.int32, padded.shape, 1)
        outside = (column_place == 0) & (nest_tile == 0) | (column_place == breadth + 1) & (
            nest_tile == nest_tiles - 1
        )
        outside = (
            outside
            | (line_place == 0) & (row_index == 0)
            | (line_place == height + 1) & (row_index == row_count - 1)
        )
        padded = jnp.where(outside & in_nest, fine_padded, padded)
        seam_cells = (column_place == breadth + 1) & (tile_index == parent_tiles - 1)
        return jnp.where(seam_cells, zero_value, padded)

    advect_scale = jnp.where(in_nest, jnp.float32(NEST_ADVECT), jnp.float32(1.0))
    mixing_scale = jnp.where(in_nest, jnp.float32(NEST_MIXING), jnp.float32(PARENT_MIXING))
    fine_first = boundary(air_state, 0)
    change = tendency(
        assemble(air_state, fine_first), wind_east, wind_north, advect_scale, mixing_scale
    )
    nudging_term = jnp.where(in_nest, NUDGING * (fine_first[:, 1:-1, 1:-1] - air_state), zero_value)
    step_one = air_state + change + nudging_term
    fine_second = boundary(step_one, 1)
    change = tendency(
        assemble(step_one, fine_second), wind_east, wind_north, advect_scale, mixing_scale
    )
    nested_two = step_one + change + NUDGING * (fine_second[:, 1:-1, 1:-1] - step_one)
    step_two = jnp.where(in_nest, nested_two, step_one)
    coarse = step_two.reshape(levels, third_y, 3, third_x, 3).mean(axis=(2, 4))
    avg_columns = jnp.arange(third_x, dtype=jnp.int32)
    avg_lines = jnp.arange(third_y, dtype=jnp.int32)
    west_last = nest_west[1]
    south_last = nest_south[1]
    place_x = (
        (west_last + (targets_x - parent_tiles) * third_x)[:, None, None]
        + avg_columns[None, :, None]
        == (first_x + columns)[None, None, :]
    ) & (targets_x >= parent_tiles)[:, None, None]
    place_x = place_x.astype(jnp.float32)
    place_y = (
        (south_last + targets_y * third_y)[:, None, None] + avg_lines[None, :, None]
        == (first_y + lines)[None, None, :]
    ).astype(jnp.float32)
    parent_y = south_last + row_index * third_y + avg_lines
    send_y = (jnp.floor_divide(parent_y, height)[None, :] == targets_y[:, None]) & in_nest
    pieces = jnp.where(send_y[:, None, :, None], coarse[None], zero_value)
    received = lax.all_to_all(pieces, "rows", split_axis=0, concat_axis=0, tiled=True)
    spread = jnp.einsum("slba,sby->lya", received, place_y, precision=highest)
    parent_x = west_last + nest_tile * third_x + avg_columns
    send_x = jnp.floor_divide(parent_x, breadth)[None, :] == targets_x[:, None]
    pieces = jnp.where(send_x[:, None, None, :], spread[None], zero_value)
    received = lax.all_to_all(pieces, "tiles", split_axis=0, concat_axis=0, tiled=True)
    placed = jnp.einsum("slya,sai->lyi", received, place_x, precision=highest)
    global_x = (first_x + columns)[None, None, :]
    global_y = (first_y + lines)[None, :, None]
    covered = (global_x >= west_last) & (global_x < west_last + nest_tiles * third_x)
    covered = covered & (global_y >= south_last) & (global_y < south_last + row_count * third_y)
    covered = covered & jnp.logical_not(in_nest)
    blended = step_two + feedback_weight[:, None, None] * (placed - step_two)
    return jnp.where(covered, blended, step_two)


LANES = 128
FIRST_LANE = 32
LAST_LANE = 96
EAST_LANE = 64
WEIGHTS = 4


def iota(shape, dim):
    return lax.broadcasted_iota(jnp.int32, shape, dim)


def split_level(place, height):
    level = ((place.astype(jnp.float32) + 0.5) * (1.0 / height)).astype(jnp.int32)
    return level, place - level * height


def table(values):
    return values.astype(jnp.float32).astype(jnp.bfloat16)


def parts_of(array):
    high = array.astype(jnp.bfloat16)
    low = (array - high.astype(jnp.float32)).astype(jnp.bfloat16)
    return high, low


def dot(left, right):
    return jnp.dot(left, right, preferred_element_type=jnp.float32)


def from_left(weights, array):
    high, low = parts_of(array)
    return dot(weights, high) + dot(weights, low)


def from_right(array, weights):
    high, low = parts_of(array)
    return dot(high, weights) + dot(low, weights)


def hat(distance):
    return jnp.maximum(0, 3 - jnp.abs(distance - 1))


def place():
    return lax.axis_index("tiles"), lax.axis_index("rows"), lax.axis_index("lev")


def level_table(levels, height):
    shape = (levels, levels * height)
    level, _ = split_level(iota(shape, 1), height)
    return table(iota(shape, 0) == level)


def spread_table(levels, height):
    shape = (levels * height, levels)
    level, _ = split_level(iota(shape, 0), height)
    return table(iota(shape, 1) == level)


def load_line(ref, levels, line):
    rows = pl.ds(line, levels, stride=ref.shape[1] // levels)
    return jnp.concatenate([ref[c, rows, :] for c in range(ref.shape[0])], axis=1)


def store_line(ref, levels, line, value):
    rows = pl.ds(line, levels, stride=ref.shape[1] // levels)
    for c in range(ref.shape[0]):
        ref[c, rows, :] = value[:, c * LANES : (c + 1) * LANES]


def load_level(ref, height, l):
    rows = pl.ds(l * height, height)
    if len(ref.shape) == 2:
        return ref[rows, :]
    return jnp.concatenate([ref[c, rows, :] for c in range(ref.shape[0])], axis=1)


def store_level(ref, height, l, value):
    rows = pl.ds(l * height, height)
    if len(ref.shape) == 2:
        ref[rows, :] = value
    else:
        for c in range(ref.shape[0]):
            ref[c, rows, :] = value[:, c * LANES : (c + 1) * LANES]


def store_slabs(ref, first, wide):
    for i in range(wide.shape[1] // LANES):
        ref[first + i] = wide[:, i * LANES : (i + 1) * LANES]


def join_slabs(ref, first, count):
    return jnp.concatenate([ref[first + i] for i in range(count)], axis=1)


def column_pieces(start, pieces):
    first = (start + 64 * LANES) // LANES - 64
    offset = start - first * LANES
    held = [(c >= 0) & (c < pieces) for c in (first, first + 1)]
    return [jnp.clip(c, 0, pieces - 1) for c in (first, first + 1)], held, offset


def pack_window(ref, field_ref, levels, top, start):
    pieces, size, _ = field_ref.shape
    height = size // levels
    slots = ref.shape[0] - 1
    lane = iota((levels, LANES), 1)
    (left, right), (left_held, right_held), offset = column_pieces(start, pieces)
    before = lax.rem(offset + LANES - 1, LANES)
    (beside, _), (beside_held, _), _ = column_pieces(start - 1, pieces)
    in_left = lane < LANES - offset
    held = jnp.where(in_left, left_held.astype(jnp.float32), right_held.astype(jnp.float32))
    west_held, east_held = beside_held.astype(jnp.float32), right_held.astype(jnp.float32)
    turn = lax.rem(LANES - offset, LANES)
    extra = jnp.zeros((levels, LANES), jnp.float32)
    for slot in range(slots):
        line = top + slot
        there = ((line >= 0) & (line < height)).astype(jnp.float32)
        rows = pl.ds(jnp.clip(line, 0, height - 1), levels, stride=height)
        near, far, west = field_ref[left, rows, :], field_ref[right, rows, :], field_ref[beside, rows, :]
        ref[slot] = jnp.where(in_left, pltpu.roll(near, turn, 1), pltpu.roll(far, turn, 1)) * (held * there)
        west = pltpu.roll(west, lax.rem(LANES + slot - before, LANES), 1) * (west_held * there)
        east = pltpu.roll(far, lax.rem(LANES + EAST_LANE + slot - offset, LANES), 1) * (east_held * there)
        extra = jnp.where(lane == slot, west, jnp.where(lane == EAST_LANE + slot, east, extra))
    ref[slots] = extra


def place_row(ref, levels, line, start, value):
    pieces, size, _ = ref.shape
    height = size // levels
    lane = iota((levels, LANES), 1)
    at, held, offset = column_pieces(start, pieces)
    value = pltpu.roll(value, offset, 1)
    there = (line >= 0) & (line < height)
    rows = pl.ds(jnp.clip(line, 0, height - 1), levels, stride=height)
    for c in range(2):
        mine = (lane >= offset) if c == 0 else (lane < offset)
        ref[at[c], rows, :] = jnp.where(mine & (held[c] & there), value, ref[at[c], rows, :])


def pack_edges(field_ref, levels):
    height = field_ref.shape[1] // levels
    lane = iota((levels, LANES), 1)
    packed = jnp.zeros((levels, LANES), jnp.float32)
    for line in range(height):
        rows = pl.ds(line, levels, stride=height)
        first = field_ref[0, rows, :]
        last = field_ref[field_ref.shape[0] - 1, rows, :]
        packed = jnp.where(lane == FIRST_LANE + line, pltpu.roll(first, FIRST_LANE + line, 1), packed)
        packed = jnp.where(lane == LAST_LANE + line, pltpu.roll(last, LAST_LANE + line + 1, 1), packed)
    return packed


def neighbour_columns(even, odd, parent_tiles, tile):
    is_odd = tile % 2 == 1
    west = jnp.where(is_odd, even, odd)
    east = jnp.where(is_odd, odd, even)
    west = jnp.where(tile == 0, jnp.zeros_like(west), west)
    east = jnp.where(tile >= parent_tiles - 1, jnp.zeros_like(east), east)
    return jnp.where(iota(west.shape, 1) < LAST_LANE, east, west)


def unpack_edges(columns, levels, height):
    wide = from_left(spread_table(levels, height), columns)
    lane = iota(wide.shape, 1)
    _, line = split_level(iota(wide.shape, 0), height)
    west = jnp.sum(jnp.where(lane == line + LAST_LANE, wide, 0.0), axis=1, keepdims=True)
    east = jnp.sum(jnp.where(lane == line + FIRST_LANE, wide, 0.0), axis=1, keepdims=True)
    return jnp.where(lane == 0, west, jnp.where(lane == 1, east, 0.0))


def refine(slabs, extra, height, breadth, row):
    slots, levels = len(slabs), extra.shape[0]
    beside = [pltpu.roll(extra, LANES - s, 1) if s else extra for s in range(slots)]
    window = jnp.concatenate([jnp.concatenate(slabs, axis=0), jnp.concatenate(beside, axis=0)], axis=1)
    shape = (2 * LANES, breadth + LANES)
    slot, cell = iota(shape, 0), iota(shape, 1)
    held = (slot <= LANES) | (slot == LANES + EAST_LANE)
    at = jnp.where(slot < LANES, slot, jnp.where(slot == LANES, -1, LANES))
    cell = jnp.where(cell == breadth, -1, jnp.where(cell == breadth + 1, breadth, cell))
    across = jnp.where(held & (cell <= breadth), hat(cell - 3 * at), 0)
    wide = from_right(window, table(across)) * (1.0 / 9.0)
    shape = (levels * height, slots * levels)
    taken = iota(shape, 1)
    slot = taken // levels
    level, line = split_level(iota(shape, 0), height)
    along = jnp.where(taken - slot * levels == level, hat(line - 3 * (slot - 1)), 0)
    cells = from_left(table(along), wide)
    ring = jnp.where(
        row == 0,
        2.0 * wide[:levels] + wide[levels : 2 * levels],
        2.0 * wide[(slots - 1) * levels :] + wide[(slots - 2) * levels : (slots - 1) * levels],
    )
    return cells, ring[:, :breadth]


def beside_rows(x, north, south):
    height = x.shape[0]
    line = iota(x.shape, 0)
    northern = jnp.where(line == 0, north, pltpu.roll(x, 1, 0))
    southern = jnp.where(line == height - 1, south, pltpu.roll(x, height - 1, 0))
    return northern, southern


def beside_columns(x, west, east):
    breadth = x.shape[1]
    column = iota(x.shape, 1)
    western = jnp.where(column == 0, west, pltpu.roll(x, 1, 1))
    eastern = jnp.where(column == breadth - 1, east, pltpu.roll(x, breadth - 1, 1))
    return western, eastern


def change_of(x, sides, u, v, upper, lower, nest):
    advect_scale = NEST_ADVECT if nest else 1.0
    mixing_scale = NEST_MIXING if nest else PARENT_MIXING
    northern, southern, western, eastern = sides
    advect = u * (eastern - western) + v * (southern - northern)
    horizontal = eastern + western + southern + northern - 4.0 * x
    vertical = upper + lower - 2.0 * x
    return -0.5 * advect_scale * advect + mixing_scale * horizontal + VERTICAL_MIX * vertical


def ghost_weight(speed, before):
    return jnp.where(before, 0.5 * NEST_ADVECT, -0.5 * NEST_ADVECT) * speed + NEST_MIXING


def full_step(out_ref, field_ref, u_ref, v_ref, level_ref, levels, lev, nest, north, south, side, fine):
    height, breadth = level_ref.shape
    zero = jnp.zeros((height, breadth), jnp.float32)

    def block(ref, l):
        return load_level(ref, height, l)

    for l in range(levels):
        x = block(field_ref, l)
        lower = block(field_ref, l - 1) if l else jnp.where(lev == 1, level_ref[...], zero)
        upper = block(field_ref, l + 1) if l < levels - 1 else jnp.where(lev == 0, level_ref[...], zero)
        rows = [0.0 if ref is None else ref[pl.ds(l, 1), :] for ref in (north, south)]
        if side is None:
            columns = (0.0, 0.0)
        else:
            beside = side[pl.ds(l * height, height), :]
            columns = (beside[:, 0:1], beside[:, 1:2])
        sides = beside_rows(x, *rows) + beside_columns(x, *columns)
        fresh = x + change_of(x, sides, block(u_ref, l), block(v_ref, l), upper, lower, nest)
        if nest:
            fresh = fresh - NUDGING * x if fine is None else fresh + NUDGING * (block(fine, l) - x)
        store_level(out_ref, height, l, fresh)


def inner_line(height, row):
    return jnp.where(row == 0, height - 1, 0)


def edge_level(ref, height, lev):
    last = ref.shape[1] // height - 1
    return jnp.where(lev == 0, load_level(ref, height, last), load_level(ref, height, 0))


def ghost_row_weights(ghost, breadth):
    cell, third = iota((breadth, 3 * LANES), 0), iota((breadth, 3 * LANES), 1)
    kind = third // LANES
    offset = cell - 3 * (third - kind * LANES)
    middle = jnp.where(offset == 1, 3, jnp.where((offset == 0) | (offset == 2), 2, 0))
    weight = jnp.where(kind == 1, middle, jnp.where(offset == kind, 1, 0))
    return from_right(ghost, table(weight)) * (1.0 / 27.0)


def ghost_column_weights(first, last, levels, height):
    shape = (levels * height, LANES)
    lane = iota(shape, 1)
    _, line = split_level(iota(shape, 0), height)
    block = lane // 8
    inside = lane - block * 8
    eastern = inside >= 3
    kind = jnp.where(eastern, inside - 3, inside)
    offset = line - 3 * block
    middle = jnp.where(offset == 1, 3, jnp.where((offset == 0) | (offset == 2), 2, 0))
    weight = jnp.where(kind == 1, middle, jnp.where(offset == kind, 1, 0))
    weight = jnp.where((inside < 6) & (block < height // 3), weight, 0).astype(jnp.float32)
    columns = jnp.where(eastern, last, first) * weight
    return from_left(level_table(levels, height), columns) * (1.0 / 27.0)


def pack_kernel(
    levels,
    west_hbm,
    south_hbm,
    weight_hbm,
    air_hbm,
    north_hbm,
    rows_ref,
    air_ref,
    west_ref,
    south_ref,
    weight_ref,
    north_ref,
    sems,
):
    pieces, size, _ = air_ref.shape
    breadth = pieces * LANES
    height = size // levels
    third_y = height // 3
    slots = rows_ref.shape[0] - 1 - pieces
    tile, row, _ = place()
    nest = tile == lax.axis_size("tiles") - 1
    inner = inner_line(height, row)

    def column_copies(source, target, first):
        return [
            pltpu.make_async_copy(source.at[:, pl.ds(c * LANES, LANES)], target.at[c], sems.at[first + c])
            for c in range(pieces)
        ]

    copies = column_copies(air_hbm, air_ref, 0)
    copies.append(pltpu.make_async_copy(west_hbm, west_ref, sems.at[2 * pieces]))
    copies.append(pltpu.make_async_copy(south_hbm, south_ref, sems.at[2 * pieces + 1]))
    copies.append(pltpu.make_async_copy(weight_hbm, weight_ref, sems.at[2 * pieces + 2]))
    speeds = column_copies(north_hbm, north_ref, pieces)
    for copy in copies:
        copy.start()

    @pl.when(nest)
    def _():
        for copy in speeds:
            copy.start()

    for copy in copies:
        copy.wait()
    store_slabs(rows_ref, slots + 1, load_line(air_ref, levels, inner))
    part = rows_ref.at[pl.ds(0, slots + 1)]

    @pl.when(nest)
    def _():
        for copy in speeds:
            copy.wait()
        part[...] = jnp.zeros_like(part)
        store_slabs(rows_ref, WEIGHTS, load_line(north_ref, levels, inner))

    @pl.when(jnp.logical_not(nest))
    def _():
        start = west_ref[0] - tile * breadth
        top = south_ref[0] - 1 - row * height
        pack_window(part, air_ref, levels, top + (1 - row) * third_y, start)


def own_kernel(
    levels, west_ref, south_ref, air_ref, east_ref, north_ref, own_ref, level_ref, speeds_ref, edges_ref
):
    pieces, size, _ = air_ref.shape
    breadth = pieces * LANES
    height = size // levels
    third_y = height // 3
    slots = own_ref.shape[0] - 1
    tile, row, lev = place()
    nest = tile == lax.axis_size("tiles") - 1
    level_ref[...] = edge_level(air_ref, height, lev)

    @pl.when(nest)
    def _():
        inner = inner_line(height, row)
        shape = (2 * levels, size)
        taken = iota(shape, 0)
        level, line = split_level(iota(shape, 1), height)
        wanted = jnp.where(taken < levels, height - 1 - inner, inner)
        picked = table((lax.rem(taken, levels) == level) & (line == wanted))
        speeds = from_left(picked, north_ref[...])
        outer = speeds[:levels]
        store_slabs(speeds_ref, 0, outer)
        store_slabs(speeds_ref, pieces, speeds[levels:])
        own_ref[...] = jnp.zeros_like(own_ref)
        edges_ref[...] = jnp.zeros_like(edges_ref)
        store_slabs(own_ref, 0, ghost_row_weights(ghost_weight(outer, row == 0), breadth))
        first = ghost_weight(east_ref[:, 0:1], True)
        last = ghost_weight(east_ref[:, breadth - 1 : breadth], False)
        own_ref[WEIGHTS - 1] = ghost_column_weights(first, last, levels, height)

    @pl.when(jnp.logical_not(nest))
    def _():
        start = west_ref[0] - tile * breadth
        top = south_ref[0] - 1 - row * height
        pack_window(own_ref, air_ref, levels, top + row * third_y, start)
        edges = pack_edges(air_ref, levels)
        edges_ref[0] = edges
        own_ref[slots] = own_ref[slots] + edges
        speeds_ref[...] = jnp.zeros_like(speeds_ref)


def set_halo(rows_ref, first, northern_ref, southern_ref, row):
    halo = join_slabs(rows_ref, first, rows_ref.shape[0] - first)
    zero = jnp.zeros_like(halo)
    northern_ref[...] = jnp.where(row == 0, zero, halo)
    southern_ref[...] = jnp.where(row == 0, halo, zero)


def parent_step(
    levels, west_ref, south_ref, shared, rows_ref, columns, field_ref, other_ref, side_ref, northern_ref, southern_ref
):
    height = side_ref.shape[0] // levels
    slots = other_ref.shape[0] - 1
    tile, row, lev = place()
    set_halo(rows_ref, slots + 1, northern_ref, southern_ref, row)
    side_ref[...] = unpack_edges(columns, levels, height)
    full_step(field_ref, *shared, levels, lev, False, northern_ref, southern_ref, side_ref, None)
    start = west_ref[1] - tile * field_ref.shape[0] * LANES
    top = south_ref[1] - 1 - row * height
    pack_window(other_ref, field_ref, levels, top + (1 - row) * (height // 3), start)


def early_kernel(
    levels,
    west_ref,
    south_ref,
    air_ref,
    east_ref,
    north_ref,
    rows_ref,
    level_ref,
    one_ref,
    field_ref,
    other_ref,
    side_ref,
    northern_ref,
    southern_ref,
):
    slots = other_ref.shape[0] - 1
    tile_count = lax.axis_size("tiles")
    tile, row, lev = place()
    shared = (air_ref, east_ref, north_ref, level_ref)

    @pl.when(tile == tile_count - 1)
    def _():
        set_halo(rows_ref, slots + 1, northern_ref, southern_ref, row)
        full_step(field_ref, *shared, levels, lev, True, northern_ref, southern_ref, None, None)
        other_ref[...] = jnp.zeros_like(other_ref)

    @pl.when(tile == 0)
    def _():
        columns = neighbour_columns(one_ref[slots], one_ref[slots], tile_count - 1, tile)
        refs = (field_ref, other_ref, side_ref, northern_ref, southern_ref)
        parent_step(levels, west_ref, south_ref, shared, rows_ref, columns, *refs)


def middle_kernel(
    levels,
    west_ref,
    south_ref,
    air_ref,
    east_ref,
    north_ref,
    rows_ref,
    level_ref,
    three_ref,
    one_ref,
    given_field_ref,
    given_other_ref,
    field_ref,
    other_ref,
    side_ref,
    northern_ref,
    southern_ref,
):
    slots = other_ref.shape[0] - 1
    tile_count = lax.axis_size("tiles")
    tile, _, _ = place()
    shared = (air_ref, east_ref, north_ref, level_ref)

    @pl.when((tile > 0) & (tile < tile_count - 1))
    def _():
        columns = neighbour_columns(one_ref[slots], three_ref[0], tile_count - 1, tile)
        refs = (field_ref, other_ref, side_ref, northern_ref, southern_ref)
        parent_step(levels, west_ref, south_ref, shared, rows_ref, columns, *refs)


def first_kernel(
    levels,
    west_ref,
    south_ref,
    early_ref,
    east_ref,
    speeds_ref,
    three_ref,
    two_ref,
    one_ref,
    field_ref,
    edge_ref,
    own_ref,
):
    pieces, size, _ = early_ref.shape
    height, breadth = edge_ref.shape
    slots = one_ref.shape[0] - 1
    tile, row, lev = place()
    nest = tile == lax.axis_size("tiles") - 1

    @pl.when(jnp.logical_not(nest))
    def _():
        edge_ref[...] = jnp.zeros_like(edge_ref)
        start = west_ref[1] - tile * breadth
        top = south_ref[1] - 1 - row * height
        pack_window(own_ref, early_ref, levels, top + row * (height // 3), start)

    @pl.when(nest)
    def _():
        slabs = [one_ref[s] + two_ref[s] + three_ref[s] for s in range(slots + 1)]
        cells, ring = refine(slabs[:slots], slabs[slots], height, breadth, row)
        lane = iota((size, LANES), 1)
        for c in range(pieces):
            piece = slice(c * LANES, (c + 1) * LANES)
            value = early_ref[c] + NUDGING * cells[:, piece]
            if c == 0:
                ghost = ghost_weight(east_ref[:, piece], True) * cells[:, breadth : breadth + 1]
                value = value + jnp.where(lane == 0, ghost, 0.0)
            if c == pieces - 1:
                ghost = ghost_weight(east_ref[:, piece], False) * cells[:, breadth + 1 : breadth + 2]
                value = value + jnp.where(lane == LANES - 1, ghost, 0.0)
            field_ref[c] = value
        outer = height - 1 - inner_line(height, row)
        ghost = ghost_weight(join_slabs(speeds_ref, 0, pieces), row == 0) * ring
        store_line(field_ref, levels, outer, load_line(field_ref, levels, outer) + ghost)
        edge_ref[...] = edge_level(field_ref, height, lev)


def average_kernel(levels, field_ref, east_ref, north_ref, rows_ref, message_ref, part_ref, nothing_ref):
    pieces, size, _ = field_ref.shape
    height, breadth = nothing_ref.shape
    third_y = height // 3
    tile, row, lev = place()

    @pl.when(tile == lax.axis_size("tiles") - 1)
    def _():
        nothing_ref[...] = jnp.zeros_like(nothing_ref)
        full_step(part_ref, field_ref, east_ref, north_ref, nothing_ref, levels, lev, True, None, None, None, None)
        sums = sums_table(breadth)
        shape = (third_y * levels, size)
        taken = iota(shape, 0)
        block = taken // levels
        level, line = split_level(iota(shape, 1), height)
        offset = line - 3 * block
        rows = table((taken - block * levels == level) & (offset >= 0) & (offset <= 2))
        means = from_left(rows, from_right(part_ref[...], sums)) * (1.0 / 9.0)
        for m in range(third_y):
            message_ref[m] = means[m * levels : (m + 1) * levels]
        shared = load_line(field_ref, levels, inner_line(height, row))
        shared = ghost_weight(join_slabs(rows_ref, WEIGHTS, pieces), row == 0) * shared
        message_ref[third_y] = from_right(shared, sums) * (1.0 / 9.0)
        for i in range(third_y + 1, message_ref.shape[0]):
            message_ref[i] = jnp.zeros((levels, LANES), jnp.float32)


def sums_table(breadth):
    offset = iota((breadth, LANES), 0) - 3 * iota((breadth, LANES), 1)
    return table((offset >= 0) & (offset <= 2))


def pack_column(slabs, extra, slot):
    lane = iota(extra.shape, 1)
    packed = jnp.where(slot == -1, extra, pltpu.roll(extra, LANES - EAST_LANE, 1))
    inside = (slot >= 0) & (slot < LANES)
    for s, slab in enumerate(slabs):
        turned = pltpu.roll(slab, lax.rem(s - slot + 64 * LANES, LANES), 1)
        packed = jnp.where((lane == s) & inside, turned, packed)
    return packed


def message_kernel(
    levels, west_ref, level_ref, part_ref, coef_ref, own_ref, other_ref, message_ref, side_ref
):
    height, breadth = level_ref.shape
    third_y = height // 3
    tile, row, lev = place()
    nest = tile == lax.axis_size("tiles") - 1

    @pl.when(jnp.logical_not(nest))
    def _():
        message_ref[...] = own_ref[...] + other_ref[...]
        slots = message_ref.shape[0] - 1
        first = tile * breadth - west_ref[1]
        lane = iota((levels, LANES), 1)
        columns = [
            pack_column([message_ref[s] for s in range(slots)], message_ref[slots], slot)
            for slot in (first, first + breadth - 1)
        ]
        side_ref[0] = jnp.where(lane < EAST_LANE, columns[0], pltpu.roll(columns[1], EAST_LANE, 1))

    @pl.when(nest)
    def _():
        offset = iota((third_y, height), 1) - 3 * iota((third_y, height), 0)
        rows = table((offset >= 0) & (offset <= 2))
        across = from_left(rows, from_right(level_ref[...], sums_table(breadth))) * (VERTICAL_MIX / 9.0)
        at_edge = iota((levels, LANES), 0) == jnp.where(lev == 0, levels - 1, 0)
        for m in range(third_y):
            message_ref[m] = part_ref[m] + jnp.where(at_edge, across[m : m + 1], 0.0)
        for i in range(third_y, message_ref.shape[0]):
            message_ref[i] = part_ref[i]
        side_ref[0] = jnp.zeros((levels, LANES), jnp.float32)

    side_ref[pl.ds(1, WEIGHTS)] = coef_ref[pl.ds(0, WEIGHTS)]


def blend_kernel(
    levels,
    western,
    west_ref,
    weight_ref,
    field_ref,
    window_ref,
    beside_ref,
    middle_ref,
    other_ref,
    coef_middle_ref,
    coef_near_ref,
    rows_ref,
):
    pieces, size, _ = field_ref.shape
    height = size // levels
    third_y = height // 3
    slots = third_y + 2
    tile_count = lax.axis_size("tiles")
    tile, row, _ = place()
    nest = tile == tile_count - 1

    @pl.when(nest)
    def _():
        store_slabs(rows_ref, 0, load_line(field_ref, levels, inner_line(height, row)))
        for i in range(pieces, rows_ref.shape[0]):
            rows_ref[i] = jnp.zeros((levels, LANES), jnp.float32)

    @pl.when(jnp.logical_not(nest))
    def _():
        paired = (tile == 1) | (tile == (0 if western else 2))

        def mine(i):
            return jnp.where(tile == 1, middle_ref[i], other_ref[i])

        def coefficient(i):
            other = beside_ref[1 + i] if western else coef_near_ref[i]
            return jnp.where(tile == 1, coef_middle_ref[i], other)

        breadth = pieces * LANES
        partner_east = tile == (0 if western else 1)
        slot = jnp.where(partner_east, (tile + 1) * breadth, tile * breadth - 1) - west_ref[1]
        column = jnp.where(partner_east, beside_ref[0], pltpu.roll(beside_ref[0], LANES - EAST_LANE, 1))
        lane = iota((levels, LANES), 1)

        def whole(s):
            return jnp.where(paired & (lane == slot), column[:, s : s + 1], window_ref[s])

        level = iota((levels, LANES), 0)
        weight = jnp.zeros((levels, LANES), jnp.float32)
        for l in range(levels):
            weight = jnp.where(level == l, weight_ref[l], weight)
        extra = window_ref[slots]
        extra = jnp.where(paired & (slot == -1) & (lane < EAST_LANE), column, extra)
        east_column = pltpu.roll(column, EAST_LANE, 1)
        extra = jnp.where(paired & (slot == LANES) & (lane >= EAST_LANE), east_column, extra)
        at_first, at_last = lane == 0, lane == LANES - 1
        lines = []
        for s in range(slots):
            x = whole(s)
            west = jnp.where(at_first, extra[:, s : s + 1], pltpu.roll(x, 1, 1))
            last = EAST_LANE + s
            east = jnp.where(at_last, extra[:, last : last + 1], pltpu.roll(x, LANES - 1, 1))
            lines.append((west, x, east))
        edges = coefficient(WEIGHTS - 1)
        ghosts = [coefficient(q) for q in range(3)]

        def outward(side, q):
            near = lines[1] if side == 0 else lines[slots - 2]
            far = lines[0] if side == 0 else lines[slots - 1]
            return (2.0 / 3.0) * far[q] + (1.0 / 3.0) * near[q]

        def sideward(s):
            west, x, east = lines[s]
            return (2.0 / 3.0) * jnp.where(at_first, west, east) + (1.0 / 3.0) * x

        sidewards = [sideward(s) for s in range(slots)]
        columns = [w + 7.0 * x + e for w, x, e in lines]
        for m in range(third_y):
            x = lines[m + 1][1]
            value = mine(m) + (NUDGING / 81.0) * (columns[m] + 7.0 * columns[m + 1] + columns[m + 2])
            for q in range(3):
                lane_of = 8 * m + q
                first, last = edges[:, lane_of : lane_of + 1], edges[:, lane_of + 3 : lane_of + 4]
                scale = jnp.where(at_first, first, jnp.where(at_last, last, 0.0))
                value = value + scale * sidewards[m + q]
            for side, at in ((0, 0), (1, third_y - 1)):
                if m == at:
                    for q in range(3):
                        value = value + jnp.where(row == side, ghosts[q], 0.0) * outward(side, q)
            rows_ref[m] = x + weight * (value - x)
        rows_ref[third_y] = weight * mine(third_y)


def later_kernel(
    levels,
    west_ref,
    south_ref,
    field_ref,
    east_ref,
    north_ref,
    level_ref,
    middle_ref,
    other_ref,
    parent_ref,
    blend_ref,
    out_ref,
    fine_ref,
    side_ref,
    northern_ref,
    southern_ref,
):
    height, breadth = level_ref.shape
    third_y = height // 3
    slots = third_y + 2
    tile, row, lev = place()
    nest = tile == lax.axis_size("tiles") - 1

    @pl.when(nest)
    def _():
        slabs = [middle_ref[s] + other_ref[s] for s in range(slots + 1)]
        cells, ring = refine(slabs[:slots], slabs[slots], height, breadth, row)
        fine_ref[...] = cells[:, :breadth]
        side_ref[...] = cells[:, breadth:]
        zero = jnp.zeros_like(ring)
        northern_ref[...] = jnp.where(row == 0, ring, zero)
        southern_ref[...] = jnp.where(row == 0, zero, ring)
        full_step(
            out_ref,
            field_ref,
            east_ref,
            north_ref,
            level_ref,
            levels,
            lev,
            True,
            northern_ref,
            southern_ref,
            side_ref,
            fine_ref,
        )

    @pl.when(jnp.logical_not(nest))
    def _():
        out_ref[...] = parent_ref[...]
        start = west_ref[1] - tile * breadth
        top = south_ref[1] + row * third_y - row * height
        for m in range(third_y):
            place_row(out_ref, levels, top + m, start, blend_ref[m])


def last_kernel(
    levels, west_ref, south_ref, given_ref, speeds_ref, blend_ref, rows_ref, out_hbm, out_ref, sems
):
    pieces, size, _ = given_ref.shape
    breadth = pieces * LANES
    height = size // levels
    third_y = height // 3
    tile, row, _ = place()
    nest = tile == lax.axis_size("tiles") - 1
    out_ref[...] = given_ref[...]

    @pl.when(nest)
    def _():
        inner = inner_line(height, row)
        halo = ghost_weight(join_slabs(speeds_ref, pieces, pieces), row == 1) * join_slabs(rows_ref, 0, pieces)
        store_line(out_ref, levels, inner, load_line(out_ref, levels, inner) + halo)

    @pl.when(jnp.logical_not(nest))
    def _():
        start = west_ref[1] - tile * breadth
        top = south_ref[1] + (1 - row) * third_y - row * height
        for m in range(third_y):
            value = rows_ref[m]
            if m == 0:
                value = value + jnp.where(row == 0, blend_ref[third_y], 0.0)
            if m == third_y - 1:
                value = value + jnp.where(row == 1, blend_ref[third_y], 0.0)
            place_row(out_ref, levels, top + m, start, value)
        near = jnp.where(row == 0, third_y - 1, 0)
        line = south_ref[1] + row * third_y - row * height + near
        place_row(out_ref, levels, line, start, blend_ref[near] + rows_ref[third_y])

    copies = [
        pltpu.make_async_copy(out_ref.at[c], out_hbm.at[:, pl.ds(c * LANES, LANES)], sems.at[c])
        for c in range(pieces)
    ]
    for copy in copies:
        copy.start()
    for copy in copies:
        copy.wait()


def call(kernel, outs, inputs, places, scratch=(), flops=0, out_place="v", aliases=()):
    spaces = {"s": pltpu.SMEM, "v": pltpu.VMEM, "h": pltpu.HBM}
    outs = [spaces[out_place](out, jnp.float32) if isinstance(out, tuple) else out for out in outs]
    moved = sum(4 * math.prod(out.shape) for out in outs) + sum(array.nbytes for array in inputs)
    inputs = [
        array if p == "v" else pltpu.with_memory_space_constraint(array, spaces[p])
        for array, p in zip(inputs, places)
    ]
    return pl.pallas_call(
        kernel,
        out_shape=outs,
        in_specs=[pl.BlockSpec(memory_space=spaces[p]) for p in places],
        out_specs=[pl.BlockSpec(memory_space=out.memory_space) for out in outs],
        scratch_shapes=[pltpu.VMEM(s, jnp.float32) if isinstance(s, tuple) else s for s in scratch],
        input_output_aliases=dict(aliases),
        compiler_params=pltpu.CompilerParams(vmem_limit_bytes=32 * 1024 * 1024),
        cost_estimate=pl.CostEstimate(flops=flops, bytes_accessed=moved, transcendentals=0),
    )(*inputs)


def per_device_paired(air_state, wind_east, wind_north, feedback_weight, nest_west, nest_south):
    levels, height, breadth = air_state.shape
    third_y = height // 3
    pieces = breadth // LANES
    slots = third_y + 2
    tile_count = lax.axis_size("tiles")
    size = levels * height
    flat = (size, breadth)
    chunked = (pieces, size, LANES)
    air, east, north = (array.reshape(flat) for array in (air_state, wind_east, wind_north))
    swap = [(0, 1), (1, 0)]

    def slabs(count):
        return (count, levels, LANES)

    def kernel(body):
        return functools.partial(body, levels)

    rows, air_pieces, west, south, weight = call(
        kernel(pack_kernel),
        [
            slabs(slots + 1 + pieces),
            chunked,
            pltpu.SMEM((2,), jnp.int32),
            pltpu.SMEM((2,), jnp.int32),
            pltpu.SMEM((levels,), jnp.float32),
        ],
        [nest_west, nest_south, feedback_weight, air, north],
        "hhhhh",
        [chunked, pltpu.SemaphoreType.DMA((2 * pieces + 3,))],
    )
    own, level, speeds, edges = call(
        kernel(own_kernel),
        [slabs(slots + 1), (height, breadth), slabs(2 * pieces), slabs(slots + 2)],
        [west, south, air_pieces, east, north],
        "ssvvv",
        flops=30 * size * breadth,
    )
    rows = lax.ppermute(rows, "rows", swap)
    level = lax.ppermute(level, "lev", swap)
    where = [(t, r, l) for t in range(tile_count) for r in range(2) for l in range(2)]
    at = {position: i for i, position in enumerate(where)}

    def over_tiles(message, step, *without):
        pairs = []
        for t, r, l in where:
            idle = t in without or (t ^ step) in without
            pairs.append((at[t, r, l], at[(t, r, 1 - l) if idle else (t ^ step, r, l)]))
        return lax.ppermute(message, ("tiles", "rows", "lev"), pairs)

    halo = over_tiles(edges, 3, 0)
    eastern = nest_west[1] > breadth
    rows, eastern = lax.optimization_barrier((rows, eastern))
    window = own + rows[: slots + 1]
    around = [(t, (t - 1) % tile_count) for t in range(tile_count)]
    starting = [
        over_tiles(window, 1),
        over_tiles(window, 2, 0),
        lax.ppermute(window, "tiles", around),
    ]
    sides = [(size, LANES), (levels, breadth), (levels, breadth)]
    early, other = call(
        kernel(early_kernel),
        [chunked, slabs(slots + 1)],
        [west, south, air, east, north, rows, level, starting[0]],
        "ssvvvvvv",
        sides,
        flops=30 * size * breadth,
    )
    early, other = call(
        kernel(middle_kernel),
        [chunked, slabs(slots + 1)],
        [west, south, air, east, north, rows, level, halo, starting[0], early, other],
        "ssvvvvvvvvv",
        sides,
        flops=30 * size * breadth,
        aliases=[(9, 0), (10, 1)],
    )
    other = lax.ppermute(other, "rows", swap)
    first, edge, own = call(
        kernel(first_kernel),
        [chunked, (height, breadth), slabs(slots + 1)],
        [west, south, early, east, speeds, *starting[::-1]],
        "ssvvvvvv",
        flops=10 * size * breadth,
    )
    level = lax.ppermute(edge, "lev", swap)
    (part,) = call(
        kernel(average_kernel),
        [slabs(slots + 1)],
        [first, east, north, rows],
        "vvvv",
        [flat, (height, breadth)],
        flops=30 * size * breadth,
    )
    message, side_message = call(
        kernel(message_kernel),
        [slabs(slots + 1), slabs(1 + WEIGHTS)],
        [west, level, part, starting[1], own, other],
        "svvvvv",
    )
    def finish(western, arrays):
        west, south, weight, first, east, north, level, message, side_message, early, speeds, coefs = arrays
        if western:
            other, beside = over_tiles(message, 3, 1), over_tiles(side_message, 1, 3)
        else:
            other, beside = over_tiles(message, 1, 0), over_tiles(side_message, 3, 0)
        middle = over_tiles(message, 2, 0)
        (blend,) = call(
            functools.partial(blend_kernel, levels, western),
            [slabs(third_y + 1)],
            [west, weight, first, message, beside, middle, other, *coefs],
            "ss" + "v" * 7,
        )
        rows = lax.ppermute(blend, "rows", swap)
        (later,) = call(
            kernel(later_kernel),
            [chunked],
            [west, south, first, east, north, level, middle, other, early, blend],
            "ss" + "v" * 8,
            [flat, *sides],
            flops=30 * size * breadth,
        )
        (out,) = call(
            kernel(last_kernel),
            [flat],
            [west, south, later, speeds, blend, rows],
            "ssvvvv",
            [chunked, pltpu.SemaphoreType.DMA((pieces,))],
            out_place="h",
        )
        return out

    arrays = (west, south, weight, first, east, north, level, message, side_message, early, speeds)
    arrays += ((starting[1], starting[0]),)
    out = lax.cond(
        eastern,
        functools.partial(finish, False),
        functools.partial(finish, True),
        arrays,
    )
    return out.reshape(air_state.shape)


def solution(mesh):
    in_specs = (
        P(("members", "lev"), "rows", "tiles"),
        P(("members", "lev"), "rows", "tiles"),
        P(("members", "lev"), "rows", "tiles"),
        P("lev"),
        P("members"),
        P("members"),
    )
    out_specs = P(("members", "lev"), "rows", "tiles")
    paired = mesh.shape["tiles"] == 4 and mesh.shape["rows"] == 2 and mesh.shape["lev"] == 2
    return jax.shard_map(
        per_device_paired if paired else per_device, mesh=mesh, in_specs=in_specs, out_specs=out_specs, check_vma=False
    )
```

profile of v0, /device:TPU:10, one launch (start us, length us, event | category | flops | bytes accessed | tf_op | source)
XLA Modules:
  0.0 31.7 jit_solution(13880409310052415381)
XLA Ops:
  0.0 1.5 %shard_map.66 = (f32[14,16,128]{2,1,0:T(8,128)S(1)}, f32[3,384,128]{2,1,0:T(8,128)S(1)}, s32[2]{0:T(128)S(4)}, s32[2]{0:T(128)S(4)}, f32[16]{0:T(128)S(4)}) custom-call(s32[2]{0:T(128)} %west_hbm.1, s32[2]{0:T(128)} %south_hbm.1, f32[16]{0:T(128)} %weight_hbm.1, f32[384,384]{1,0:T(8,128)} %bitcast.6, f32[384,384]{1,0:T(8,128)} %bitcast.9), custom_call_target="tpu_custom_call" | custom-call | bytes 1884320 | tf_op jit(solution)/shard_map/pallas_call | solution.py:977
  1.5 0.6 %collective-permute-start.8 = (f32[14,16,128]{2,1,0:T(8,128)S(1)}, f32[14,16,128]{2,1,0:T(8,128)S(1)}, u32[]{:S(2)}, u32[]{:S(2)}) collective-permute-start(f32[14,16,128]{2,1,0:T(8,128)S(1)} %get-tuple-element.107), channel_id=1, source_target_pairs={{0,2},{2,0},{1,3},{3,1},{4,6},{6,4},{5,7},{7,5},{8,10},{10,8},{9,1... | collective-permute-start | bytes 344072 | tf_op jit(solution)/shard_map/ppermute | solution.py:1027
  2.1 0.3 shard_map.67
  2.5 1.6 %collective-permute-start.10 = (f32[12,16,128]{2,1,0:T(8,128)S(1)}, f32[12,16,128]{2,1,0:T(8,128)S(1)}, u32[]{:S(2)}, u32[]{:S(2)}) collective-permute-start(f32[12,16,128]{2,1,0:T(8,128)S(1)} %get-tuple-element.114), channel_id=1, source_target_pairs={{0,1},{1,0},{2,3},{3,2},{4,8},{5,9},{6,10},{7,11},{8,4},{9,5},{10,... | collective-permute-start | bytes 294920 | tf_op jit(solution)/shard_map/ppermute | solution.py:1037
  4.1 0.6 %slice.6 = s32[1]{0:T(128)} slice(s32[2]{0:T(128)S(1)} %copy-done.3), slice={[1:2]} | slice | bytes 8 | tf_op jit(solution)/shard_map/slice | solution.py:1040
  5.3 1.1 %collective-permute-done.8.rows_ref = f32[14,16,128]{2,1,0:T(8,128)S(1)} collective-permute-done((f32[14,16,128]{2,1,0:T(8,128)S(1)}, f32[14,16,128]{2,1,0:T(8,128)S(1)}, u32[]{:S(2)}, u32[]{:S(2)}) %collective-permute-start.8) | collective-permute-done | bytes 114720 | tf_op jit(solution)/shard_map/ppermute | solution.py:1027
  6.5 0.5 %collective-permute-start.11 = (f32[11,16,128]{2,1,0:T(8,128)S(1)}, f32[11,16,128]{2,1,0:T(8,128)S(1)}, u32[]{:S(2)}, u32[]{:S(2)}) collective-permute-start(f32[11,16,128]{2,1,0:T(8,128)S(1)} %slice_add_fusion), channel_id=1, source_target_pairs={{0,4},{1,5},{2,6},{3,7},{4,0},{5,1},{6,2},{7,3},{8,12},{9,13},{10,... | collective-permute-start | bytes 270344 | tf_op jit(solution)/shard_map/ppermute | solution.py:1037
  7.0 2.6 %collective-permute-start.13 = (f32[11,16,128]{2,1,0:T(8,128)S(1)}, f32[11,16,128]{2,1,0:T(8,128)S(1)}, u32[]{:S(2)}, u32[]{:S(2)}) collective-permute-start(f32[11,16,128]{2,1,0:T(8,128)S(1)} %slice_add_fusion), channel_id=1, source_target_pairs={{0,1},{1,0},{2,3},{3,2},{4,12},{5,13},{6,14},{7,15},{8,9},{9,8},{1... | collective-permute-start | bytes 270344 | tf_op jit(solution)/shard_map/ppermute | solution.py:1037
  9.6 1.5 %collective-permute-done.11.one_ref = f32[11,16,128]{2,1,0:T(8,128)S(1)} collective-permute-done((f32[11,16,128]{2,1,0:T(8,128)S(1)}, f32[11,16,128]{2,1,0:T(8,128)S(1)}, u32[]{:S(2)}, u32[]{:S(2)}) %collective-permute-start.11) | collective-permute-done | bytes 90144 | tf_op jit(solution)/shard_map/ppermute | solution.py:1037
  11.1 1.1 %shard_map.69 = (f32[3,384,128]{2,1,0:T(8,128)S(1)}, f32[11,16,128]{2,1,0:T(8,128)S(1)}) custom-call(s32[2]{0:T(128)S(4)} %get-tuple-element.109.west_ref, s32[2]{0:T(128)S(4)} %get-tuple-element.110.south_ref, f32[384,384]{1,0:T(8,128)S(1)} %bitcast.8, f32[384,384]{1,0:T(8,128)S(1)} %bitcast.18, ...), custom_call_target="tpu_custom_call", output_to_operand_aliasing={{0}: (9, {}), {1}: (10, {})} | custom-call | flops 4423680 | bytes 3469328 | tf_op jit(solution)/shard_map/pallas_call | solution.py:977
  12.2 0.6 %collective-permute-start.15 = (f32[11,16,128]{2,1,0:T(8,128)S(1)}, f32[11,16,128]{2,1,0:T(8,128)S(1)}, u32[]{:S(2)}, u32[]{:S(2)}) collective-permute-start(f32[11,16,128]{2,1,0:T(8,128)S(1)} %get-tuple-element.123), channel_id=1, source_target_pairs={{0,2},{2,0},{1,3},{3,1},{4,6},{6,4},{5,7},{7,5},{8,10},{10,8},{9,1... | collective-permute-start | bytes 270344 | tf_op jit(solution)/shard_map/ppermute | solution.py:1067
  12.8 2.2 %collective-permute-done.13.two_ref.coef_ref = f32[11,16,128]{2,1,0:T(8,128)S(1)} collective-permute-done((f32[11,16,128]{2,1,0:T(8,128)S(1)}, f32[11,16,128]{2,1,0:T(8,128)S(1)}, u32[]{:S(2)}, u32[]{:S(2)}) %collective-permute-start.13) | collective-permute-done | bytes 90144 | tf_op jit(solution)/shard_map/ppermute | solution.py:1037
  15.0 0.5 %collective-permute-done.12.three_ref = f32[11,16,128]{2,1,0:T(8,128)S(1)} collective-permute-done((f32[11,16,128]{2,1,0:T(8,128)S(1)}, f32[11,16,128]{2,1,0:T(8,128)S(1)}, u32[]{:S(2)}, u32[]{:S(2)}) %collective-permute-start.12) | collective-permute-done | bytes 90144 | tf_op jit(solution)/shard_map/ppermute | solution.py:1047
  15.5 0.2 shard_map.70
  15.8 1.2 %collective-permute-done.14.level_ref = f32[24,384]{1,0:T(8,128)S(1)} collective-permute-done((f32[24,384]{1,0:T(8,128)S(1)}, f32[24,384]{1,0:T(8,128)S(1)}, u32[]{:S(2)}, u32[]{:S(2)}) %collective-permute-start.14) | collective-permute-done | bytes 36896 | tf_op jit(solution)/shard_map/ppermute | solution.py:1075
  17.1 14.5 %conditional.1 = (f32[16,24,384]{2,1,0:T(8,128)}) conditional(s32[]{:T(128)} %convert_element_type.3, (f32[11,16,128]{2,1,0:T(8,128)S(1)}, f32[5,16,128]{2,1,0:T(8,128)S(1)}, s32[2]{0:T(128)S(4)}, f32[16]{0:T(128)S(4)}, f32[3,384,128]{2,1,0:T(8,128)S(1)}, /*index=5*/f32[11,16,128]{2,1,0:T(8,128)S(1)}, f32[11,16,128]{2,1,0:T(8,128)S(1)}, ...), branch_computations={%region_0.0_spmd, %region_1.0_spmd} | conditional | flops 4423680 | bytes 6951184 | solution.py:1124
  17.1 0.2 collective-permute-start.5
  17.4 3.7 %collective-permute-start.4 = (f32[11,16,128]{2,1,0:T(8,128)S(1)}, f32[11,16,128]{2,1,0:T(8,128)S(1)}, u32[]{:S(2)}, u32[]{:S(2)}) collective-permute-start(f32[11,16,128]{2,1,0:T(8,128)S(1)} %get-tuple-element.80.window_ref), channel_id=1, source_target_pairs={{0,1},{1,0},{2,3},{3,2},{4,12},{5,13},{6,14},{7,15},{8,9},{9,8},{1... | collective-permute-start | bytes 270344 | tf_op jit(solution)/shard_map/cond/branch_1_fun/ppermute | solution.py:1037
  21.0 4.7 %collective-permute-done.6.beside_ref = f32[5,16,128]{2,1,0:T(8,128)S(1)} collective-permute-done((f32[5,16,128]{2,1,0:T(8,128)S(1)}, f32[5,16,128]{2,1,0:T(8,128)S(1)}, u32[]{:S(2)}, u32[]{:S(2)}) %collective-permute-start.6) | collective-permute-done | bytes 40992 | tf_op jit(solution)/shard_map/cond/branch_1_fun/ppermute | solution.py:1037
  25.7 0.5 %branch_1_fun.3.blend_ref = f32[9,16,128]{2,1,0:T(8,128)S(1)} custom-call(s32[2]{0:T(128)S(4)} %get-tuple-element.74.west_ref, f32[16]{0:T(128)S(4)} %get-tuple-element.82.weight_ref, f32[3,384,128]{2,1,0:T(8,128)S(1)} %get-tuple-element.76.field_ref, f32[11,16,128]{2,1,0:T(8,128)S(1)} %get-tuple-element.80.window_ref, ...), custom_call_target="tpu_custom_call" | custom-call | bytes 1155144 | tf_op jit(solution)/shard_map/cond/branch_1_fun/pallas_call | solution.py:977
  26.2 0.6 %collective-permute-start.7 = (f32[9,16,128]{2,1,0:T(8,128)S(1)}, f32[9,16,128]{2,1,0:T(8,128)S(1)}, u32[]{:S(2)}, u32[]{:S(2)}) collective-permute-start(f32[9,16,128]{2,1,0:T(8,128)S(1)} %branch_1_fun.3.blend_ref), channel_id=1, source_target_pairs={{0,2},{2,0},{1,3},{3,1},{4,6},{6,4},{5,7},{7,5},{8,10},{10,8},{9,1... | collective-permute-start | bytes 221192 | tf_op jit(solution)/shard_map/cond/branch_1_fun/ppermute | solution.py:1103
  26.8 0.2 branch_1_fun.4.given_ref
  27.0 3.6 %collective-permute-done.7.rows_ref = f32[9,16,128]{2,1,0:T(8,128)S(1)} collective-permute-done((f32[9,16,128]{2,1,0:T(8,128)S(1)}, f32[9,16,128]{2,1,0:T(8,128)S(1)}, u32[]{:S(2)}, u32[]{:S(2)}) %collective-permute-start.7) | collective-permute-done | bytes 73760 | tf_op jit(solution)/shard_map/cond/branch_1_fun/ppermute | solution.py:1103
  30.6 1.0 %branch_1_fun.5 = f32[384,384]{1,0:T(8,128)} custom-call(s32[2]{0:T(128)S(4)} %get-tuple-element.74.west_ref, s32[2]{0:T(128)S(4)} %get-tuple-element.75.south_ref, f32[3,384,128]{2,1,0:T(8,128)S(1)} %branch_1_fun.4.given_ref, f32[6,16,128]{2,1,0:T(8,128)S(1)} %get-tuple-element.86.speeds_ref, f32[9,16,128]{2,1,0:T(8,128)S(1)} %branch_1_fun.3.blend_ref, ...), custom_call_target="tpu_custom_call" | custom-call | bytes 1376272 | tf_op jit(solution)/shard_map/cond/branch_1_fun/pallas_call | solution.py:977
  (21 shorter events, 0.3 us)
Async XLA Ops:
  0.0 2.1 %copy-start.1 = (f32[16,24,384]{2,1,0:T(8,128)S(1)}, f32[16,24,384]{2,1,0:T(8,128)}, u32[]{:S(2)}) copy-start(f32[16,24,384]{2,1,0:T(8,128)} %param.10) | copy-start | bytes 1769476
  0.0 2.1 %copy-start.2 = (f32[16,24,384]{2,1,0:T(8,128)S(1)}, f32[16,24,384]{2,1,0:T(8,128)}, u32[]{:S(2)}) copy-start(f32[16,24,384]{2,1,0:T(8,128)} %param.9) | copy-start | bytes 1769476
  1.5 5.0 %collective-permute-start.8 = (f32[14,16,128]{2,1,0:T(8,128)S(1)}, f32[14,16,128]{2,1,0:T(8,128)S(1)}, u32[]{:S(2)}, u32[]{:S(2)}) collective-permute-start(f32[14,16,128]{2,1,0:T(8,128)S(1)} %get-tuple-element.107), channel_id=1, source_target_pairs={{0,2},{2,0},{1,3},{3,1},{4,6},{6,4},{5,7},{7,5},{8,10},{10,8},{9,1... | collective-permute-start | bytes 344072 | tf_op jit(solution)/shard_map/ppermute | solution.py:1027
  2.1 9.0 %copy-start = (f32[16,24,384]{2,1,0:T(8,128)S(1)}, f32[16,24,384]{2,1,0:T(8,128)}, u32[]{:S(2)}) copy-start(f32[16,24,384]{2,1,0:T(8,128)} %param.8) | copy-start | bytes 1769476
  2.4 1.7 %copy-start.3 = (s32[2]{0:T(128)S(1)}, s32[2]{0:T(128)}, u32[]{:S(2)}) copy-start(s32[2]{0:T(128)} %west_hbm.1) | copy-start | bytes 28
  2.5 8.6 %collective-permute-start.10 = (f32[12,16,128]{2,1,0:T(8,128)S(1)}, f32[12,16,128]{2,1,0:T(8,128)S(1)}, u32[]{:S(2)}, u32[]{:S(2)}) collective-permute-start(f32[12,16,128]{2,1,0:T(8,128)S(1)} %get-tuple-element.114), channel_id=1, source_target_pairs={{0,1},{1,0},{2,3},{3,2},{4,8},{5,9},{6,10},{7,11},{8,4},{9,5},{10,... | collective-permute-start | bytes 294920 | tf_op jit(solution)/shard_map/ppermute | solution.py:1037
  6.5 4.6 %collective-permute-start.11 = (f32[11,16,128]{2,1,0:T(8,128)S(1)}, f32[11,16,128]{2,1,0:T(8,128)S(1)}, u32[]{:S(2)}, u32[]{:S(2)}) collective-permute-start(f32[11,16,128]{2,1,0:T(8,128)S(1)} %slice_add_fusion), channel_id=1, source_target_pairs={{0,4},{1,5},{2,6},{3,7},{4,0},{5,1},{6,2},{7,3},{8,12},{9,13},{10,... | collective-permute-start | bytes 270344 | tf_op jit(solution)/shard_map/ppermute | solution.py:1037
  7.0 2.6 %collective-permute-start.9 = (f32[24,384]{1,0:T(8,128)S(1)}, f32[24,384]{1,0:T(8,128)S(1)}, u32[]{:S(2)}, u32[]{:S(2)}) collective-permute-start(f32[24,384]{1,0:T(8,128)S(1)} %get-tuple-element.113), channel_id=1, source_target_pairs={{0,1},{1,0},{2,3},{3,2},{4,5},{5,4},{6,7},{7,6},{8,9},{9,8},{10,11... | collective-permute-start | bytes 110600 | tf_op jit(solution)/shard_map/ppermute | solution.py:1028
  7.0 8.0 %collective-permute-start.13 = (f32[11,16,128]{2,1,0:T(8,128)S(1)}, f32[11,16,128]{2,1,0:T(8,128)S(1)}, u32[]{:S(2)}, u32[]{:S(2)}) collective-permute-start(f32[11,16,128]{2,1,0:T(8,128)S(1)} %slice_add_fusion), channel_id=1, source_target_pairs={{0,1},{1,0},{2,3},{3,2},{4,12},{5,13},{6,14},{7,15},{8,9},{9,8},{1... | collective-permute-start | bytes 270344 | tf_op jit(solution)/shard_map/ppermute | solution.py:1037
  9.6 5.9 %collective-permute-start.12 = (f32[11,16,128]{2,1,0:T(8,128)S(1)}, f32[11,16,128]{2,1,0:T(8,128)S(1)}, u32[]{:S(2)}, u32[]{:S(2)}) collective-permute-start(f32[11,16,128]{2,1,0:T(8,128)S(1)} %slice_add_fusion), channel_id=1, source_target_pairs={{0,12},{4,0},{8,4},{12,8},{1,13},{5,1},{9,5},{13,9},{2,14},{6,2},{... | collective-permute-start | bytes 270344 | tf_op jit(solution)/shard_map/ppermute | solution.py:1047
  12.2 4.8 %collective-permute-start.15 = (f32[11,16,128]{2,1,0:T(8,128)S(1)}, f32[11,16,128]{2,1,0:T(8,128)S(1)}, u32[]{:S(2)}, u32[]{:S(2)}) collective-permute-start(f32[11,16,128]{2,1,0:T(8,128)S(1)} %get-tuple-element.123), channel_id=1, source_target_pairs={{0,2},{2,0},{1,3},{3,1},{4,6},{6,4},{5,7},{7,5},{8,10},{10,8},{9,1... | collective-permute-start | bytes 270344 | tf_op jit(solution)/shard_map/ppermute | solution.py:1067
  15.7 1.3 %collective-permute-start.14 = (f32[24,384]{1,0:T(8,128)S(1)}, f32[24,384]{1,0:T(8,128)S(1)}, u32[]{:S(2)}, u32[]{:S(2)}) collective-permute-start(f32[24,384]{1,0:T(8,128)S(1)} %get-tuple-element.120), channel_id=1, source_target_pairs={{0,1},{1,0},{2,3},{3,2},{4,5},{5,4},{6,7},{7,6},{8,9},{9,8},{10,11... | collective-permute-start | bytes 110600 | tf_op jit(solution)/shard_map/ppermute | solution.py:1075
  17.1 8.6 %collective-permute-start.5 = (f32[11,16,128]{2,1,0:T(8,128)S(1)}, f32[11,16,128]{2,1,0:T(8,128)S(1)}, u32[]{:S(2)}, u32[]{:S(2)}) collective-permute-start(f32[11,16,128]{2,1,0:T(8,128)S(1)} %get-tuple-element.80.window_ref), channel_id=1, source_target_pairs={{0,1},{1,0},{2,3},{3,2},{4,5},{5,4},{6,7},{7,6},{8,12},{9,13},{10,... | collective-permute-start | bytes 270344 | tf_op jit(solution)/shard_map/cond/branch_1_fun/ppermute | solution.py:1037
  17.4 8.3 %collective-permute-start.4 = (f32[11,16,128]{2,1,0:T(8,128)S(1)}, f32[11,16,128]{2,1,0:T(8,128)S(1)}, u32[]{:S(2)}, u32[]{:S(2)}) collective-permute-start(f32[11,16,128]{2,1,0:T(8,128)S(1)} %get-tuple-element.80.window_ref), channel_id=1, source_target_pairs={{0,1},{1,0},{2,3},{3,2},{4,12},{5,13},{6,14},{7,15},{8,9},{9,8},{1... | collective-permute-start | bytes 270344 | tf_op jit(solution)/shard_map/cond/branch_1_fun/ppermute | solution.py:1037
  21.0 4.7 %collective-permute-start.6 = (f32[5,16,128]{2,1,0:T(8,128)S(1)}, f32[5,16,128]{2,1,0:T(8,128)S(1)}, u32[]{:S(2)}, u32[]{:S(2)}) collective-permute-start(f32[5,16,128]{2,1,0:T(8,128)S(1)} %get-tuple-element.83), channel_id=1, source_target_pairs={{0,1},{1,0},{2,3},{3,2},{4,8},{5,9},{6,10},{7,11},{8,4},{9,5},{10,... | collective-permute-start | bytes 122888 | tf_op jit(solution)/shard_map/cond/branch_1_fun/ppermute | solution.py:1037
  26.2 4.4 %collective-permute-start.7 = (f32[9,16,128]{2,1,0:T(8,128)S(1)}, f32[9,16,128]{2,1,0:T(8,128)S(1)}, u32[]{:S(2)}, u32[]{:S(2)}) collective-permute-start(f32[9,16,128]{2,1,0:T(8,128)S(1)} %branch_1_fun.3.blend_ref), channel_id=1, source_target_pairs={{0,2},{2,0},{1,3},{3,1},{4,6},{6,4},{5,7},{7,5},{8,10},{10,8},{9,1... | collective-permute-start | bytes 221192 | tf_op jit(solution)/shard_map/cond/branch_1_fun/ppermute | solution.py:1103
where the time goes:
time: 31.8 us; the launch traced here: 31.7 us
  waiting for transfers between devices  14.9 us (47%)
  starting transfers between devices  10.5 us (33%)
  Pallas kernels  4.96 us (16%)
  between operations  0.72 us (2%)
  local copies, waits for them, and re-layouts  0.6 us (2%)
    ppermute x6, starting transfers between devices, over_tiles(): return lax.ppermute(message, ('tiles', 'rows', 'lev'), pairs)  8.61 us
    ppermute x6, waiting for transfers between devices, over_tiles(): return lax.ppermute(message, ('tiles', 'rows', 'lev'), pairs)  8.35 us
    pallas_call x10, Pallas kernels, call(): pl.pallas_call(kernel, out_shape=outs, in_specs=[pl.BlockSpec(memory_spac...  4.96 us
    ppermute x1, waiting for transfers between devices, finish(): rows = lax.ppermute(blend, 'rows', swap)  3.64 us
    ppermute x1, waiting for transfers between devices, per_device_paired(): level = lax.ppermute(edge, 'lev', swap)  1.18 us
    ppermute x1, waiting for transfers between devices, per_device_paired(): rows = lax.ppermute(rows, 'rows', swap)  1.14 us
  transfers between devices with their start and end apart: 12, of which 7 were waited for; matrix products, arithmetic and copies ran while one was open for 2% of the time, Pallas kernels for 6%

commit v1 on v0

--- a/solution.py
+++ b/solution.py
@@ -557,6 +557,7 @@
         top = south_ref[0] - 1 - row * height
         pack_window(own_ref, air_ref, levels, top + row * third_y, start)
         edges = pack_edges(air_ref, levels)
+        edges_ref[...] = jnp.zeros_like(edges_ref)
         edges_ref[0] = edges
         own_ref[slots] = own_ref[slots] + edges
         speeds_ref[...] = jnp.zeros_like(speeds_ref)
@@ -739,7 +740,7 @@
 
 
 def message_kernel(
-    levels, west_ref, level_ref, part_ref, coef_ref, own_ref, other_ref, message_ref, side_ref
+    levels, west_ref, level_ref, part_ref, coef_ref, own_ref, other_ref, message_ref, far_ref, side_ref
 ):
     height, breadth = level_ref.shape
     third_y = height // 3
@@ -749,6 +750,9 @@
     @pl.when(jnp.logical_not(nest))
     def _():
         message_ref[...] = own_ref[...] + other_ref[...]
+        far_ref[pl.ds(0, message_ref.shape[0])] = message_ref[...]
+        for i in range(message_ref.shape[0], far_ref.shape[0]):
+            far_ref[i] = jnp.zeros((levels, LANES), jnp.float32)
         slots = message_ref.shape[0] - 1
         first = tile * breadth - west_ref[1]
         lane = iota((levels, LANES), 1)
@@ -756,7 +760,7 @@
             pack_column([message_ref[s] for s in range(slots)], message_ref[slots], slot)
             for slot in (first, first + breadth - 1)
         ]
-        side_ref[0] = jnp.where(lane < EAST_LANE, columns[0], pltpu.roll(columns[1], EAST_LANE, 1))
+        side_ref[...] = jnp.where(lane < EAST_LANE, columns[0], pltpu.roll(columns[1], EAST_LANE, 1))
 
     @pl.when(nest)
     def _():
@@ -768,9 +772,9 @@
             message_ref[m] = part_ref[m] + jnp.where(at_edge, across[m : m + 1], 0.0)
         for i in range(third_y, message_ref.shape[0]):
             message_ref[i] = part_ref[i]
-        side_ref[0] = jnp.zeros((levels, LANES), jnp.float32)
-
-    side_ref[pl.ds(1, WEIGHTS)] = coef_ref[pl.ds(0, WEIGHTS)]
+        far_ref[pl.ds(0, third_y + 1)] = message_ref[pl.ds(0, third_y + 1)]
+        far_ref[pl.ds(third_y + 1, WEIGHTS)] = coef_ref[pl.ds(0, WEIGHTS)]
+        side_ref[...] = jnp.zeros_like(side_ref)
 
 
 def blend_kernel(
@@ -809,13 +813,13 @@
             return jnp.where(tile == 1, middle_ref[i], other_ref[i])
 
         def coefficient(i):
-            other = beside_ref[1 + i] if western else coef_near_ref[i]
+            other = other_ref[third_y + 1 + i] if western else coef_near_ref[i]
             return jnp.where(tile == 1, coef_middle_ref[i], other)
 
         breadth = pieces * LANES
         partner_east = tile == (0 if western else 1)
         slot = jnp.where(partner_east, (tile + 1) * breadth, tile * breadth - 1) - west_ref[1]
-        column = jnp.where(partner_east, beside_ref[0], pltpu.roll(beside_ref[0], LANES - EAST_LANE, 1))
+        column = jnp.where(partner_east, beside_ref[...], pltpu.roll(beside_ref[...], LANES - EAST_LANE, 1))
         lane = iota((levels, LANES), 1)
 
         def whole(s):
@@ -927,13 +931,12 @@
 def last_kernel(
     levels, west_ref, south_ref, given_ref, speeds_ref, blend_ref, rows_ref, out_hbm, out_ref, sems
 ):
-    pieces, size, _ = given_ref.shape
+    pieces, size, _ = out_ref.shape
     breadth = pieces * LANES
     height = size // levels
     third_y = height // 3
     tile, row, _ = place()
     nest = tile == lax.axis_size("tiles") - 1
-    out_ref[...] = given_ref[...]
 
     @pl.when(nest)
     def _():
@@ -966,9 +969,9 @@
         copy.wait()
 
 
-def call(kernel, outs, inputs, places, scratch=(), flops=0, out_place="v", aliases=()):
+def call(kernel, outs, inputs, places, scratch=(), flops=0, aliases=()):
     spaces = {"s": pltpu.SMEM, "v": pltpu.VMEM, "h": pltpu.HBM}
-    outs = [spaces[out_place](out, jnp.float32) if isinstance(out, tuple) else out for out in outs]
+    outs = [pltpu.VMEM(out, jnp.float32) if isinstance(out, tuple) else out for out in outs]
     moved = sum(4 * math.prod(out.shape) for out in outs) + sum(array.nbytes for array in inputs)
     inputs = [
         array if p == "v" else pltpu.with_memory_space_constraint(array, spaces[p])
@@ -1040,6 +1043,7 @@
     eastern = nest_west[1] > breadth
     rows, eastern = lax.optimization_barrier((rows, eastern))
     window = own + rows[: slots + 1]
+    own_0 = own
     around = [(t, (t - 1) % tile_count) for t in range(tile_count)]
     starting = [
         over_tiles(window, 1),
@@ -1081,16 +1085,16 @@
         [flat, (height, breadth)],
         flops=30 * size * breadth,
     )
-    message, side_message = call(
+    message, far_message, side_message = call(
         kernel(message_kernel),
-        [slabs(slots + 1), slabs(1 + WEIGHTS)],
-        [west, level, part, starting[1], own, other],
+        [slabs(slots + 1), slabs(third_y + 1 + WEIGHTS), (levels, LANES)],
+        [west, level, part, own_0, own, other],
         "svvvvv",
     )
     def finish(western, arrays):
-        west, south, weight, first, east, north, level, message, side_message, early, speeds, coefs = arrays
+        west, south, weight, first, east, north, level, message, far_message, side_message, early, speeds, coefs = arrays
         if western:
-            other, beside = over_tiles(message, 3, 1), over_tiles(side_message, 1, 3)
+            other, beside = over_tiles(far_message, 3, 1), over_tiles(side_message, 1, 3)
         else:
             other, beside = over_tiles(message, 1, 0), over_tiles(side_message, 3, 0)
         middle = over_tiles(message, 2, 0)
@@ -1109,17 +1113,17 @@
             [flat, *sides],
             flops=30 * size * breadth,
         )
-        (out,) = call(
+        out, _ = call(
             kernel(last_kernel),
-            [flat],
+            [pltpu.HBM(flat, jnp.float32), chunked],
             [west, south, later, speeds, blend, rows],
             "ssvvvv",
-            [chunked, pltpu.SemaphoreType.DMA((pieces,))],
-            out_place="h",
+            [pltpu.SemaphoreType.DMA((pieces,))],
+            aliases=[(2, 1)],
         )
         return out
 
-    arrays = (west, south, weight, first, east, north, level, message, side_message, early, speeds)
+    arrays = (west, south, weight, first, east, north, level, message, far_message, side_message, early, speeds)
     arrays += ((starting[1], starting[0]),)
     out = lax.cond(
         eastern,

time: 31.8 us -> 32.5 us (1.022)
  the two profiles are of different devices: /device:TPU:10 before, /device:TPU:0 now
where the time goes in v1:
time: 32.5 us; the launch traced here: 32.4 us
  starting transfers between devices  15.9 us (49%)
  waiting for transfers between devices  9.53 us (29%)
  Pallas kernels  4.96 us (15%)
  local copies, waits for them, and re-layouts  1.16 us (4%)
  between operations  0.74 us (2%)
    ppermute x6, starting transfers between devices, over_tiles(): return lax.ppermute(message, ('tiles', 'rows', 'lev'), pairs)  7.43 us
    pallas_call x10, Pallas kernels, call(): pl.pallas_call(kernel, out_shape=outs, in_specs=[pl.BlockSpec(memory_spac...  4.96 us
    ppermute x6, waiting for transfers between devices, over_tiles(): return lax.ppermute(message, ('tiles', 'rows', 'lev'), pairs)  3.36 us
    ppermute x1, starting transfers between devices, per_device_paired(): rows = lax.ppermute(rows, 'rows', swap)  3 us
    ppermute x1, waiting for transfers between devices, finish(): rows = lax.ppermute(blend, 'rows', swap)  2.68 us
    ppermute x1, starting transfers between devices, per_device_paired(): lax.ppermute(window, 'tiles', around)  2.05 us
    ppermute x1, starting transfers between devices, per_device_paired(): other = lax.ppermute(other, 'rows', swap)  1.81 us
    ppermute x1, starting transfers between devices, finish(): rows = lax.ppermute(blend, 'rows', swap)  1.56 us
  transfers between devices with their start and end apart: 12, of which 7 were waited for; matrix products, arithmetic and copies ran while one was open for 2% of the time, Pallas kernels for 5%

profile of v1, /device:TPU:0, one launch (start us, length us, event | category | flops | bytes accessed | tf_op | source)
XLA Modules:
  0.0 32.4 jit_solution(13349864594298760037)
XLA Ops:
  0.0 1.5 %shard_map.66 = (f32[14,16,128]{2,1,0:T(8,128)S(1)}, f32[3,384,128]{2,1,0:T(8,128)S(1)}, s32[2]{0:T(128)S(4)}, s32[2]{0:T(128)S(4)}, f32[16]{0:T(128)S(4)}) custom-call(s32[2]{0:T(128)} %west_hbm.1, s32[2]{0:T(128)} %south_hbm.1, f32[16]{0:T(128)} %weight_hbm.1, f32[384,384]{1,0:T(8,128)} %bitcast.6, f32[384,384]{1,0:T(8,128)} %bitcast.9), custom_call_target="tpu_custom_call" | custom-call | bytes 1884320 | tf_op jit(solution)/shard_map/pallas_call | solution.py:980
  1.5 3.0 %collective-permute-start.8 = (f32[14,16,128]{2,1,0:T(8,128)S(1)}, f32[14,16,128]{2,1,0:T(8,128)S(1)}, u32[]{:S(2)}, u32[]{:S(2)}) collective-permute-start(f32[14,16,128]{2,1,0:T(8,128)S(1)} %get-tuple-element.112), channel_id=1, source_target_pairs={{0,2},{2,0},{1,3},{3,1},{4,6},{6,4},{5,7},{7,5},{8,10},{10,8},{9,1... | collective-permute-start | bytes 344072 | tf_op jit(solution)/shard_map/ppermute | solution.py:1030
  4.5 0.3 shard_map.67
  4.9 0.6 %copy-done.3 = s32[2]{0:T(128)S(1)} copy-done((s32[2]{0:T(128)S(1)}, s32[2]{0:T(128)}, u32[]{:S(2)}) %copy-start.3) | copy-done | bytes 32
  5.5 0.6 %slice.6 = s32[1]{0:T(128)} slice(s32[2]{0:T(128)S(1)} %copy-done.3), slice={[1:2]} | slice | bytes 8 | tf_op jit(solution)/shard_map/slice | solution.py:1043
  6.7 0.9 %collective-permute-done.8.rows_ref = f32[14,16,128]{2,1,0:T(8,128)S(1)} collective-permute-done((f32[14,16,128]{2,1,0:T(8,128)S(1)}, f32[14,16,128]{2,1,0:T(8,128)S(1)}, u32[]{:S(2)}, u32[]{:S(2)}) %collective-permute-start.8) | collective-permute-done | bytes 114720 | tf_op jit(solution)/shard_map/ppermute | solution.py:1030
  7.7 1.9 %collective-permute-start.11 = (f32[11,16,128]{2,1,0:T(8,128)S(1)}, f32[11,16,128]{2,1,0:T(8,128)S(1)}, u32[]{:S(2)}, u32[]{:S(2)}) collective-permute-start(f32[11,16,128]{2,1,0:T(8,128)S(1)} %slice_add_fusion), channel_id=1, source_target_pairs={{0,4},{1,5},{2,6},{3,7},{4,0},{5,1},{6,2},{7,3},{8,12},{9,13},{10,... | collective-permute-start | bytes 270344 | tf_op jit(solution)/shard_map/ppermute | solution.py:1040
  9.6 0.5 %collective-permute-start.13 = (f32[11,16,128]{2,1,0:T(8,128)S(1)}, f32[11,16,128]{2,1,0:T(8,128)S(1)}, u32[]{:S(2)}, u32[]{:S(2)}) collective-permute-start(f32[11,16,128]{2,1,0:T(8,128)S(1)} %slice_add_fusion), channel_id=1, source_target_pairs={{0,1},{1,0},{2,3},{3,2},{4,12},{5,13},{6,14},{7,15},{8,9},{9,8},{1... | collective-permute-start | bytes 270344 | tf_op jit(solution)/shard_map/ppermute | solution.py:1040
  10.1 2.1 %collective-permute-start.12 = (f32[11,16,128]{2,1,0:T(8,128)S(1)}, f32[11,16,128]{2,1,0:T(8,128)S(1)}, u32[]{:S(2)}, u32[]{:S(2)}) collective-permute-start(f32[11,16,128]{2,1,0:T(8,128)S(1)} %slice_add_fusion), channel_id=1, source_target_pairs={{0,12},{4,0},{8,4},{12,8},{1,13},{5,1},{9,5},{13,9},{2,14},{6,2},{... | collective-permute-start | bytes 270344 | tf_op jit(solution)/shard_map/ppermute | solution.py:1051
  12.3 1.1 %shard_map.68 = (f32[3,384,128]{2,1,0:T(8,128)S(1)}, f32[11,16,128]{2,1,0:T(8,128)S(1)}) custom-call(s32[2]{0:T(128)S(4)} %get-tuple-element.114.west_ref, s32[2]{0:T(128)S(4)} %get-tuple-element.115.south_ref, f32[384,384]{1,0:T(8,128)S(1)} %bitcast.7, f32[384,384]{1,0:T(8,128)S(1)} %bitcast.17, f32[384,384]{1,0:T(8,128)S(1)} %bitcast.11, ...), custom_call_target="tpu_custom_call" | custom-call | flops 4423680 | bytes 2691088 | tf_op jit(solution)/shard_map/pallas_call | solution.py:980
  13.4 1.8 %collective-permute-start.15 = (f32[11,16,128]{2,1,0:T(8,128)S(1)}, f32[11,16,128]{2,1,0:T(8,128)S(1)}, u32[]{:S(2)}, u32[]{:S(2)}) collective-permute-start(f32[11,16,128]{2,1,0:T(8,128)S(1)} %get-tuple-element.128), channel_id=1, source_target_pairs={{0,2},{2,0},{1,3},{3,1},{4,6},{6,4},{5,7},{7,5},{8,10},{10,8},{9,1... | collective-permute-start | bytes 270344 | tf_op jit(solution)/shard_map/ppermute | solution.py:1071
  15.2 0.4 %collective-permute-done.12.three_ref = f32[11,16,128]{2,1,0:T(8,128)S(1)} collective-permute-done((f32[11,16,128]{2,1,0:T(8,128)S(1)}, f32[11,16,128]{2,1,0:T(8,128)S(1)}, u32[]{:S(2)}, u32[]{:S(2)}) %collective-permute-start.12) | collective-permute-done | bytes 90144 | tf_op jit(solution)/shard_map/ppermute | solution.py:1051
  15.6 0.2 shard_map.70
  15.9 1.2 %collective-permute-done.14.level_ref = f32[24,384]{1,0:T(8,128)S(1)} collective-permute-done((f32[24,384]{1,0:T(8,128)S(1)}, f32[24,384]{1,0:T(8,128)S(1)}, u32[]{:S(2)}, u32[]{:S(2)}) %collective-permute-start.14) | collective-permute-done | bytes 36896 | tf_op jit(solution)/shard_map/ppermute | solution.py:1079
  17.1 1.0 %collective-permute-done.15.other_ref = f32[11,16,128]{2,1,0:T(8,128)S(1)} collective-permute-done((f32[11,16,128]{2,1,0:T(8,128)S(1)}, f32[11,16,128]{2,1,0:T(8,128)S(1)}, u32[]{:S(2)}, u32[]{:S(2)}) %collective-permute-start.15) | collective-permute-done | bytes 90144 | tf_op jit(solution)/shard_map/ppermute | solution.py:1071
  18.2 14.1 %conditional.1 = (f32[16,24,384]{2,1,0:T(8,128)}) conditional(s32[]{:T(128)} %convert_element_type.3, (f32[11,16,128]{2,1,0:T(8,128)S(1)}, f32[13,16,128]{2,1,0:T(8,128)S(1)}, f32[16,128]{1,0:T(8,128)S(1)}, s32[2]{0:T(128)S(4)}, f32[16]{0:T(128)S(4)}, /*index=5*/f32[3,384,128]{2,1,0:T(8,128)S(1)}, f32[11,16,128]{2,1,0:T(8,128)S(1)}, ...), branch_computations={%region_0.0_spmd, %region_1.0_spmd} | conditional | flops 4423680 | bytes 7475472 | solution.py:1128
  18.2 4.3 %collective-permute-start.1 = (f32[13,16,128]{2,1,0:T(8,128)S(1)}, f32[13,16,128]{2,1,0:T(8,128)S(1)}, u32[]{:S(2)}, u32[]{:S(2)}) collective-permute-start(f32[13,16,128]{2,1,0:T(8,128)S(1)} %get-tuple-element.69), channel_id=1, source_target_pairs={{0,12},{1,13},{2,14},{3,15},{4,5},{5,4},{6,7},{7,6},{8,9},{9,8},{1... | collective-permute-start | bytes 319496 | tf_op jit(solution)/shard_map/cond/branch_0_fun/ppermute | solution.py:1040
  22.7 0.5 %collective-permute-start.2 = (f32[16,128]{1,0:T(8,128)S(1)}, f32[16,128]{1,0:T(8,128)S(1)}, u32[]{:S(2)}, u32[]{:S(2)}) collective-permute-start(f32[16,128]{1,0:T(8,128)S(1)} %get-tuple-element.72), channel_id=1, source_target_pairs={{0,4},{1,5},{2,6},{3,7},{4,0},{5,1},{6,2},{7,3},{8,9},{9,8},{10,11... | collective-permute-start | bytes 24584 | tf_op jit(solution)/shard_map/cond/branch_0_fun/ppermute | solution.py:1040
  23.2 3.2 %collective-permute-done.2.beside_ref = f32[16,128]{1,0:T(8,128)S(1)} collective-permute-done((f32[16,128]{1,0:T(8,128)S(1)}, f32[16,128]{1,0:T(8,128)S(1)}, u32[]{:S(2)}, u32[]{:S(2)}) %collective-permute-start.2) | collective-permute-done | bytes 8224 | tf_op jit(solution)/shard_map/cond/branch_0_fun/ppermute | solution.py:1040
  26.4 0.5 %branch_0_fun.3.blend_ref = f32[9,16,128]{2,1,0:T(8,128)S(1)} custom-call(s32[2]{0:T(128)S(4)} %get-tuple-element.62.west_ref, f32[16]{0:T(128)S(4)} %get-tuple-element.71.weight_ref, f32[3,384,128]{2,1,0:T(8,128)S(1)} %get-tuple-element.64.field_ref, f32[11,16,128]{2,1,0:T(8,128)S(1)} %get-tuple-element.68.window_ref, ...), custom_call_target="tpu_custom_call" | custom-call | bytes 1138760 | tf_op jit(solution)/shard_map/cond/branch_0_fun/pallas_call | solution.py:980
  26.9 1.6 %collective-permute-start.3 = (f32[9,16,128]{2,1,0:T(8,128)S(1)}, f32[9,16,128]{2,1,0:T(8,128)S(1)}, u32[]{:S(2)}, u32[]{:S(2)}) collective-permute-start(f32[9,16,128]{2,1,0:T(8,128)S(1)} %branch_0_fun.3.blend_ref), channel_id=1, source_target_pairs={{0,2},{2,0},{1,3},{3,1},{4,6},{6,4},{5,7},{7,5},{8,10},{10,8},{9,1... | collective-permute-start | bytes 221192 | tf_op jit(solution)/shard_map/cond/branch_0_fun/ppermute | solution.py:1107
  28.5 0.2 branch_0_fun.4.given_ref
  28.7 2.7 %collective-permute-done.3.rows_ref = f32[9,16,128]{2,1,0:T(8,128)S(1)} collective-permute-done((f32[9,16,128]{2,1,0:T(8,128)S(1)}, f32[9,16,128]{2,1,0:T(8,128)S(1)}, u32[]{:S(2)}, u32[]{:S(2)}) %collective-permute-start.3) | collective-permute-done | bytes 73760 | tf_op jit(solution)/shard_map/cond/branch_0_fun/ppermute | solution.py:1107
  31.3 1.0 %branch_0_fun.5 = (f32[384,384]{1,0:T(8,128)}, f32[3,384,128]{2,1,0:T(8,128)S(1)}) custom-call(s32[2]{0:T(128)S(4)} %get-tuple-element.62.west_ref, s32[2]{0:T(128)S(4)} %get-tuple-element.63.south_ref, f32[3,384,128]{2,1,0:T(8,128)S(1)} %branch_0_fun.4.given_ref, f32[6,16,128]{2,1,0:T(8,128)S(1)} %get-tuple-element.75.speeds_ref, ...), custom_call_target="tpu_custom_call", output_to_operand_aliasing={{1}: (2, {})} | custom-call | bytes 1966096 | tf_op jit(solution)/shard_map/cond/branch_0_fun/pallas_call | solution.py:980
  (21 shorter events, 0.7 us)
Async XLA Ops:
  0.0 4.5 %copy-start.1 = (f32[16,24,384]{2,1,0:T(8,128)S(1)}, f32[16,24,384]{2,1,0:T(8,128)}, u32[]{:S(2)}) copy-start(f32[16,24,384]{2,1,0:T(8,128)} %param.10) | copy-start | bytes 1769476
  0.0 4.5 %copy-start.2 = (f32[16,24,384]{2,1,0:T(8,128)S(1)}, f32[16,24,384]{2,1,0:T(8,128)}, u32[]{:S(2)}) copy-start(f32[16,24,384]{2,1,0:T(8,128)} %param.9) | copy-start | bytes 1769476
  1.5 6.1 %collective-permute-start.8 = (f32[14,16,128]{2,1,0:T(8,128)S(1)}, f32[14,16,128]{2,1,0:T(8,128)S(1)}, u32[]{:S(2)}, u32[]{:S(2)}) collective-permute-start(f32[14,16,128]{2,1,0:T(8,128)S(1)} %get-tuple-element.112), channel_id=1, source_target_pairs={{0,2},{2,0},{1,3},{3,1},{4,6},{6,4},{5,7},{7,5},{8,10},{10,8},{9,1... | collective-permute-start | bytes 344072 | tf_op jit(solution)/shard_map/ppermute | solution.py:1030
  4.5 7.8 %copy-start = (f32[16,24,384]{2,1,0:T(8,128)S(1)}, f32[16,24,384]{2,1,0:T(8,128)}, u32[]{:S(2)}) copy-start(f32[16,24,384]{2,1,0:T(8,128)} %param.8) | copy-start | bytes 1769476
  4.8 0.7 %copy-start.3 = (s32[2]{0:T(128)S(1)}, s32[2]{0:T(128)}, u32[]{:S(2)}) copy-start(s32[2]{0:T(128)} %west_hbm.1) | copy-start | bytes 28
  4.9 8.5 %collective-permute-start.10 = (f32[12,16,128]{2,1,0:T(8,128)S(1)}, f32[12,16,128]{2,1,0:T(8,128)S(1)}, u32[]{:S(2)}, u32[]{:S(2)}) collective-permute-start(f32[12,16,128]{2,1,0:T(8,128)S(1)} %get-tuple-element.119), channel_id=1, source_target_pairs={{0,1},{1,0},{2,3},{3,2},{4,8},{5,9},{6,10},{7,11},{8,4},{9,5},{10,... | collective-permute-start | bytes 294920 | tf_op jit(solution)/shard_map/ppermute | solution.py:1040
  7.7 4.6 %collective-permute-start.11 = (f32[11,16,128]{2,1,0:T(8,128)S(1)}, f32[11,16,128]{2,1,0:T(8,128)S(1)}, u32[]{:S(2)}, u32[]{:S(2)}) collective-permute-start(f32[11,16,128]{2,1,0:T(8,128)S(1)} %slice_add_fusion), channel_id=1, source_target_pairs={{0,4},{1,5},{2,6},{3,7},{4,0},{5,1},{6,2},{7,3},{8,12},{9,13},{10,... | collective-permute-start | bytes 270344 | tf_op jit(solution)/shard_map/ppermute | solution.py:1040
  9.6 2.6 %collective-permute-start.9 = (f32[24,384]{1,0:T(8,128)S(1)}, f32[24,384]{1,0:T(8,128)S(1)}, u32[]{:S(2)}, u32[]{:S(2)}) collective-permute-start(f32[24,384]{1,0:T(8,128)S(1)} %get-tuple-element.118), channel_id=1, source_target_pairs={{0,1},{1,0},{2,3},{3,2},{4,5},{5,4},{6,7},{7,6},{8,9},{9,8},{10,11... | collective-permute-start | bytes 110600 | tf_op jit(solution)/shard_map/ppermute | solution.py:1031
  9.6 5.7 %collective-permute-start.13 = (f32[11,16,128]{2,1,0:T(8,128)S(1)}, f32[11,16,128]{2,1,0:T(8,128)S(1)}, u32[]{:S(2)}, u32[]{:S(2)}) collective-permute-start(f32[11,16,128]{2,1,0:T(8,128)S(1)} %slice_add_fusion), channel_id=1, source_target_pairs={{0,1},{1,0},{2,3},{3,2},{4,12},{5,13},{6,14},{7,15},{8,9},{9,8},{1... | collective-permute-start | bytes 270344 | tf_op jit(solution)/shard_map/ppermute | solution.py:1040
  10.1 5.5 %collective-permute-start.12 = (f32[11,16,128]{2,1,0:T(8,128)S(1)}, f32[11,16,128]{2,1,0:T(8,128)S(1)}, u32[]{:S(2)}, u32[]{:S(2)}) collective-permute-start(f32[11,16,128]{2,1,0:T(8,128)S(1)} %slice_add_fusion), channel_id=1, source_target_pairs={{0,12},{4,0},{8,4},{12,8},{1,13},{5,1},{9,5},{13,9},{2,14},{6,2},{... | collective-permute-start | bytes 270344 | tf_op jit(solution)/shard_map/ppermute | solution.py:1051
  13.4 4.6 %collective-permute-start.15 = (f32[11,16,128]{2,1,0:T(8,128)S(1)}, f32[11,16,128]{2,1,0:T(8,128)S(1)}, u32[]{:S(2)}, u32[]{:S(2)}) collective-permute-start(f32[11,16,128]{2,1,0:T(8,128)S(1)} %get-tuple-element.128), channel_id=1, source_target_pairs={{0,2},{2,0},{1,3},{3,1},{4,6},{6,4},{5,7},{7,5},{8,10},{10,8},{9,1... | collective-permute-start | bytes 270344 | tf_op jit(solution)/shard_map/ppermute | solution.py:1071
  15.8 1.3 %collective-permute-start.14 = (f32[24,384]{1,0:T(8,128)S(1)}, f32[24,384]{1,0:T(8,128)S(1)}, u32[]{:S(2)}, u32[]{:S(2)}) collective-permute-start(f32[24,384]{1,0:T(8,128)S(1)} %get-tuple-element.125), channel_id=1, source_target_pairs={{0,1},{1,0},{2,3},{3,2},{4,5},{5,4},{6,7},{7,6},{8,9},{9,8},{10,11... | collective-permute-start | bytes 110600 | tf_op jit(solution)/shard_map/ppermute | solution.py:1079
  18.2 8.2 %collective-permute-start.1 = (f32[13,16,128]{2,1,0:T(8,128)S(1)}, f32[13,16,128]{2,1,0:T(8,128)S(1)}, u32[]{:S(2)}, u32[]{:S(2)}) collective-permute-start(f32[13,16,128]{2,1,0:T(8,128)S(1)} %get-tuple-element.69), channel_id=1, source_target_pairs={{0,12},{1,13},{2,14},{3,15},{4,5},{5,4},{6,7},{7,6},{8,9},{9,8},{1... | collective-permute-start | bytes 319496 | tf_op jit(solution)/shard_map/cond/branch_0_fun/ppermute | solution.py:1040
  22.6 3.9 %collective-permute-start = (f32[11,16,128]{2,1,0:T(8,128)S(1)}, f32[11,16,128]{2,1,0:T(8,128)S(1)}, u32[]{:S(2)}, u32[]{:S(2)}) collective-permute-start(f32[11,16,128]{2,1,0:T(8,128)S(1)} %get-tuple-element.68.window_ref), channel_id=1, source_target_pairs={{0,1},{1,0},{2,3},{3,2},{4,12},{5,13},{6,14},{7,15},{8,9},{9,8},{1... | collective-permute-start | bytes 270344 | tf_op jit(solution)/shard_map/cond/branch_0_fun/ppermute | solution.py:1040
  22.7 3.7 %collective-permute-start.2 = (f32[16,128]{1,0:T(8,128)S(1)}, f32[16,128]{1,0:T(8,128)S(1)}, u32[]{:S(2)}, u32[]{:S(2)}) collective-permute-start(f32[16,128]{1,0:T(8,128)S(1)} %get-tuple-element.72), channel_id=1, source_target_pairs={{0,4},{1,5},{2,6},{3,7},{4,0},{5,1},{6,2},{7,3},{8,9},{9,8},{10,11... | collective-permute-start | bytes 24584 | tf_op jit(solution)/shard_map/cond/branch_0_fun/ppermute | solution.py:1040
  26.9 4.4 %collective-permute-start.3 = (f32[9,16,128]{2,1,0:T(8,128)S(1)}, f32[9,16,128]{2,1,0:T(8,128)S(1)}, u32[]{:S(2)}, u32[]{:S(2)}) collective-permute-start(f32[9,16,128]{2,1,0:T(8,128)S(1)} %branch_0_fun.3.blend_ref), channel_id=1, source_target_pairs={{0,2},{2,0},{1,3},{3,1},{4,6},{6,4},{5,7},{7,5},{8,10},{10,8},{9,1... | collective-permute-start | bytes 221192 | tf_op jit(solution)/shard_map/cond/branch_0_fun/ppermute | solution.py:1107

commit v2 on v1

--- a/solution.py
+++ b/solution.py
@@ -570,83 +570,55 @@
     southern_ref[...] = jnp.where(row == 0, halo, zero)
 
 
-def parent_step(
-    levels, west_ref, south_ref, shared, rows_ref, columns, field_ref, other_ref, side_ref, northern_ref, southern_ref
-):
-    height = side_ref.shape[0] // levels
-    slots = other_ref.shape[0] - 1
-    tile, row, lev = place()
-    set_halo(rows_ref, slots + 1, northern_ref, southern_ref, row)
-    side_ref[...] = unpack_edges(columns, levels, height)
-    full_step(field_ref, *shared, levels, lev, False, northern_ref, southern_ref, side_ref, None)
-    start = west_ref[1] - tile * field_ref.shape[0] * LANES
-    top = south_ref[1] - 1 - row * height
-    pack_window(other_ref, field_ref, levels, top + (1 - row) * (height // 3), start)
-
-
 def early_kernel(
     levels,
-    west_ref,
-    south_ref,
     air_ref,
     east_ref,
     north_ref,
     rows_ref,
     level_ref,
-    one_ref,
     field_ref,
-    other_ref,
-    side_ref,
     northern_ref,
     southern_ref,
 ):
+    tile, row, lev = place()
+    nest = tile == lax.axis_size("tiles") - 1
+    set_halo(rows_ref, rows_ref.shape[0] - field_ref.shape[0], northern_ref, southern_ref, row)
+    shared = (field_ref, air_ref, east_ref, north_ref, level_ref, levels, lev)
+
+    @pl.when(nest)
+    def _():
+        full_step(*shared, True, northern_ref, southern_ref, None, None)
+
+    @pl.when(jnp.logical_not(nest))
+    def _():
+        full_step(*shared, False, northern_ref, southern_ref, None, None)
+
+
+def middle_kernel(levels, west_ref, south_ref, east_ref, three_ref, one_ref, given_ref, field_ref, other_ref):
+    pieces, size, _ = field_ref.shape
+    height, breadth = size // levels, pieces * LANES
     slots = other_ref.shape[0] - 1
     tile_count = lax.axis_size("tiles")
-    tile, row, lev = place()
-    shared = (air_ref, east_ref, north_ref, level_ref)
-
-    @pl.when(tile == tile_count - 1)
-    def _():
-        set_halo(rows_ref, slots + 1, northern_ref, southern_ref, row)
-        full_step(field_ref, *shared, levels, lev, True, northern_ref, southern_ref, None, None)
+    tile, row, _ = place()
+    nest = tile == tile_count - 1
+
+    @pl.when(nest)
+    def _():
         other_ref[...] = jnp.zeros_like(other_ref)
 
-    @pl.when(tile == 0)
-    def _():
-        columns = neighbour_columns(one_ref[slots], one_ref[slots], tile_count - 1, tile)
-        refs = (field_ref, other_ref, side_ref, northern_ref, southern_ref)
-        parent_step(levels, west_ref, south_ref, shared, rows_ref, columns, *refs)
-
-
-def middle_kernel(
-    levels,
-    west_ref,
-    south_ref,
-    air_ref,
-    east_ref,
-    north_ref,
-    rows_ref,
-    level_ref,
-    three_ref,
-    one_ref,
-    given_field_ref,
-    given_other_ref,
-    field_ref,
-    other_ref,
-    side_ref,
-    northern_ref,
-    southern_ref,
-):
-    slots = other_ref.shape[0] - 1
-    tile_count = lax.axis_size("tiles")
-    tile, _, _ = place()
-    shared = (air_ref, east_ref, north_ref, level_ref)
-
-    @pl.when((tile > 0) & (tile < tile_count - 1))
+    @pl.when(jnp.logical_not(nest))
     def _():
         columns = neighbour_columns(one_ref[slots], three_ref[0], tile_count - 1, tile)
-        refs = (field_ref, other_ref, side_ref, northern_ref, southern_ref)
-        parent_step(levels, west_ref, south_ref, shared, rows_ref, columns, *refs)
+        side = unpack_edges(columns, levels, height)
+        lane = iota((size, LANES), 1)
+        west = (0.5 * east_ref[:, pl.ds(0, LANES)] + PARENT_MIXING) * side[:, 0:1]
+        field_ref[0] = field_ref[0] + jnp.where(lane == 0, west, 0.0)
+        east = (-0.5 * east_ref[:, pl.ds(breadth - LANES, LANES)] + PARENT_MIXING) * side[:, 1:2]
+        field_ref[pieces - 1] = field_ref[pieces - 1] + jnp.where(lane == LANES - 1, east, 0.0)
+        start = west_ref[1] - tile * breadth
+        top = south_ref[1] - 1 - row * height
+        pack_window(other_ref, field_ref, levels, top + (1 - row) * (height // 3), start)
 
 
 def first_kernel(
@@ -1051,22 +1023,21 @@
         lax.ppermute(window, "tiles", around),
     ]
     sides = [(size, LANES), (levels, breadth), (levels, breadth)]
-    early, other = call(
+    (early,) = call(
         kernel(early_kernel),
-        [chunked, slabs(slots + 1)],
-        [west, south, air, east, north, rows, level, starting[0]],
-        "ssvvvvvv",
-        sides,
+        [chunked],
+        [air, east, north, rows, level],
+        "vvvvv",
+        sides[1:],
         flops=30 * size * breadth,
     )
     early, other = call(
         kernel(middle_kernel),
         [chunked, slabs(slots + 1)],
-        [west, south, air, east, north, rows, level, halo, starting[0], early, other],
-        "ssvvvvvvvvv",
-        sides,
-        flops=30 * size * breadth,
-        aliases=[(9, 0), (10, 1)],
+        [west, south, east, halo, starting[0], early],
+        "ssvvvv",
+        flops=10 * size * breadth,
+        aliases=[(5, 0)],
     )
     other = lax.ppermute(other, "rows", swap)
     first, edge, own = call(

time: 32.5 us -> 32.5 us (level)
  transfers between devices with their start and end apart: 12 -> 12, of which waited for: 7 -> 6; matrix products, arithmetic and copies ran while one was open for 2% -> 2% of each run, Pallas kernels for 5% -> 6%
where the time goes in v2:
time: 32.5 us; the launch traced here: 32.4 us
  starting transfers between devices  15.8 us (49%)
  waiting for transfers between devices  9.52 us (29%)
  Pallas kernels  5.09 us (16%)
  local copies, waits for them, and re-layouts  1.16 us (4%)
  between operations  0.75 us (2%)
    ppermute x6, starting transfers between devices, over_tiles(): return lax.ppermute(message, ('tiles', 'rows', 'lev'), pairs)  7.32 us
    pallas_call x10, Pallas kernels, call(): pl.pallas_call(kernel, out_shape=outs, in_specs=[pl.BlockSpec(memory_spac...  5.09 us
    ppermute x6, waiting for transfers between devices, over_tiles(): return lax.ppermute(message, ('tiles', 'rows', 'lev'), pairs)  3.24 us
    ppermute x1, starting transfers between devices, per_device_paired(): rows = lax.ppermute(rows, 'rows', swap)  3 us
    ppermute x1, waiting for transfers between devices, finish(): rows = lax.ppermute(blend, 'rows', swap)  2.68 us
    ppermute x1, starting transfers between devices, per_device_paired(): lax.ppermute(window, 'tiles', around)  2.05 us
    ppermute x1, starting transfers between devices, per_device_paired(): other = lax.ppermute(other, 'rows', swap)  1.81 us
    ppermute x1, starting transfers between devices, finish(): rows = lax.ppermute(blend, 'rows', swap)  1.56 us
  transfers between devices with their start and end apart: 12, of which 6 were waited for; matrix products, arithmetic and copies ran while one was open for 2% of the time, Pallas kernels for 6%

profile of v2, /device:TPU:0, one launch (start us, length us, event | category | flops | bytes accessed | tf_op | source)
XLA Modules:
  0.0 32.4 jit_solution(10811684532513701895)
XLA Ops:
  0.0 1.5 %shard_map.66 = (f32[14,16,128]{2,1,0:T(8,128)S(1)}, f32[3,384,128]{2,1,0:T(8,128)S(1)}, s32[2]{0:T(128)S(4)}, s32[2]{0:T(128)S(4)}, f32[16]{0:T(128)S(4)}) custom-call(s32[2]{0:T(128)} %west_hbm.1, s32[2]{0:T(128)} %south_hbm.1, f32[16]{0:T(128)} %weight_hbm.1, f32[384,384]{1,0:T(8,128)} %bitcast.6, f32[384,384]{1,0:T(8,128)} %bitcast.15), custom_call_target="tpu_custom_call" | custom-call | bytes 1884320 | tf_op jit(solution)/shard_map/pallas_call | solution.py:952
  1.5 3.0 %collective-permute-start.8 = (f32[14,16,128]{2,1,0:T(8,128)S(1)}, f32[14,16,128]{2,1,0:T(8,128)S(1)}, u32[]{:S(2)}, u32[]{:S(2)}) collective-permute-start(f32[14,16,128]{2,1,0:T(8,128)S(1)} %get-tuple-element.110), channel_id=1, source_target_pairs={{0,2},{2,0},{1,3},{3,1},{4,6},{6,4},{5,7},{7,5},{8,10},{10,8},{9,1... | collective-permute-start | bytes 344072 | tf_op jit(solution)/shard_map/ppermute | solution.py:1002
  4.5 0.3 shard_map.67
  4.9 0.6 %copy-done.3 = s32[2]{0:T(128)S(1)} copy-done((s32[2]{0:T(128)S(1)}, s32[2]{0:T(128)}, u32[]{:S(2)}) %copy-start.3) | copy-done | bytes 32
  5.5 0.6 %slice.6 = s32[1]{0:T(128)} slice(s32[2]{0:T(128)S(1)} %copy-done.3), slice={[1:2]} | slice | bytes 8 | tf_op jit(solution)/shard_map/slice | solution.py:1015
  6.7 0.9 %collective-permute-done.8.rows_ref = f32[14,16,128]{2,1,0:T(8,128)S(1)} collective-permute-done((f32[14,16,128]{2,1,0:T(8,128)S(1)}, f32[14,16,128]{2,1,0:T(8,128)S(1)}, u32[]{:S(2)}, u32[]{:S(2)}) %collective-permute-start.8) | collective-permute-done | bytes 114720 | tf_op jit(solution)/shard_map/ppermute | solution.py:1002
  7.7 1.9 %collective-permute-start.10 = (f32[11,16,128]{2,1,0:T(8,128)S(1)}, f32[11,16,128]{2,1,0:T(8,128)S(1)}, u32[]{:S(2)}, u32[]{:S(2)}) collective-permute-start(f32[11,16,128]{2,1,0:T(8,128)S(1)} %slice_add_fusion), channel_id=1, source_target_pairs={{0,4},{1,5},{2,6},{3,7},{4,0},{5,1},{6,2},{7,3},{8,12},{9,13},{10,... | collective-permute-start | bytes 270344 | tf_op jit(solution)/shard_map/ppermute | solution.py:1012
  9.6 0.5 %collective-permute-start.13 = (f32[11,16,128]{2,1,0:T(8,128)S(1)}, f32[11,16,128]{2,1,0:T(8,128)S(1)}, u32[]{:S(2)}, u32[]{:S(2)}) collective-permute-start(f32[11,16,128]{2,1,0:T(8,128)S(1)} %slice_add_fusion), channel_id=1, source_target_pairs={{0,1},{1,0},{2,3},{3,2},{4,12},{5,13},{6,14},{7,15},{8,9},{9,8},{1... | collective-permute-start | bytes 270344 | tf_op jit(solution)/shard_map/ppermute | solution.py:1012
  10.1 2.1 %collective-permute-start.12 = (f32[11,16,128]{2,1,0:T(8,128)S(1)}, f32[11,16,128]{2,1,0:T(8,128)S(1)}, u32[]{:S(2)}, u32[]{:S(2)}) collective-permute-start(f32[11,16,128]{2,1,0:T(8,128)S(1)} %slice_add_fusion), channel_id=1, source_target_pairs={{0,12},{4,0},{8,4},{12,8},{1,13},{5,1},{9,5},{13,9},{2,14},{6,2},{... | collective-permute-start | bytes 270344 | tf_op jit(solution)/shard_map/ppermute | solution.py:1023
  12.2 0.6 %shard_map.68.given_ref = f32[3,384,128]{2,1,0:T(8,128)S(1)} custom-call(f32[384,384]{1,0:T(8,128)S(1)} %bitcast.7, f32[384,384]{1,0:T(8,128)S(1)} %bitcast.9, f32[384,384]{1,0:T(8,128)S(1)} %bitcast.17, f32[14,16,128]{2,1,0:T(8,128)S(1)} %collective-permute-done.8.rows_ref, f32[24,384]{1,0:T(8,128)S(1)} %collective-permute-done.11.level_ref), custom_call_target="tpu_custom_call" | custom-call | flops 4423680 | bytes 2510848 | tf_op jit(solution)/shard_map/pallas_call | solution.py:952
  12.8 0.7 %shard_map.69 = (f32[3,384,128]{2,1,0:T(8,128)S(1)}, f32[11,16,128]{2,1,0:T(8,128)S(1)}) custom-call(s32[2]{0:T(128)S(4)} %get-tuple-element.112.west_ref, s32[2]{0:T(128)S(4)} %get-tuple-element.113.south_ref, f32[384,384]{1,0:T(8,128)S(1)} %bitcast.10, f32[12,16,128]{2,1,0:T(8,128)S(1)} %collective-permute-done.9.three_ref, ...), custom_call_target="tpu_custom_call", output_to_operand_aliasing={{0}: (5, {})} | custom-call | flops 1474560 | bytes 2048016 | tf_op jit(solution)/shard_map/pallas_call | solution.py:952
  13.4 1.8 %collective-permute-start.15 = (f32[11,16,128]{2,1,0:T(8,128)S(1)}, f32[11,16,128]{2,1,0:T(8,128)S(1)}, u32[]{:S(2)}, u32[]{:S(2)}) collective-permute-start(f32[11,16,128]{2,1,0:T(8,128)S(1)} %get-tuple-element.124), channel_id=1, source_target_pairs={{0,2},{2,0},{1,3},{3,1},{4,6},{6,4},{5,7},{7,5},{8,10},{10,8},{9,1... | collective-permute-start | bytes 270344 | tf_op jit(solution)/shard_map/ppermute | solution.py:1042
  15.3 0.4 %collective-permute-done.12.three_ref = f32[11,16,128]{2,1,0:T(8,128)S(1)} collective-permute-done((f32[11,16,128]{2,1,0:T(8,128)S(1)}, f32[11,16,128]{2,1,0:T(8,128)S(1)}, u32[]{:S(2)}, u32[]{:S(2)}) %collective-permute-start.12) | collective-permute-done | bytes 90144 | tf_op jit(solution)/shard_map/ppermute | solution.py:1023
  15.9 1.2 %collective-permute-done.14.level_ref = f32[24,384]{1,0:T(8,128)S(1)} collective-permute-done((f32[24,384]{1,0:T(8,128)S(1)}, f32[24,384]{1,0:T(8,128)S(1)}, u32[]{:S(2)}, u32[]{:S(2)}) %collective-permute-start.14) | collective-permute-done | bytes 36896 | tf_op jit(solution)/shard_map/ppermute | solution.py:1050
  17.1 1.1 %collective-permute-done.15.other_ref = f32[11,16,128]{2,1,0:T(8,128)S(1)} collective-permute-done((f32[11,16,128]{2,1,0:T(8,128)S(1)}, f32[11,16,128]{2,1,0:T(8,128)S(1)}, u32[]{:S(2)}, u32[]{:S(2)}) %collective-permute-start.15) | collective-permute-done | bytes 90144 | tf_op jit(solution)/shard_map/ppermute | solution.py:1042
  18.4 14.0 %conditional.1 = (f32[16,24,384]{2,1,0:T(8,128)}) conditional(s32[]{:T(128)} %convert_element_type.3, (f32[11,16,128]{2,1,0:T(8,128)S(1)}, f32[13,16,128]{2,1,0:T(8,128)S(1)}, f32[16,128]{1,0:T(8,128)S(1)}, s32[2]{0:T(128)S(4)}, f32[16]{0:T(128)S(4)}, /*index=5*/f32[3,384,128]{2,1,0:T(8,128)S(1)}, f32[11,16,128]{2,1,0:T(8,128)S(1)}, ...), branch_computations={%region_0.0_spmd, %region_1.0_spmd} | conditional | flops 4423680 | bytes 7475472 | solution.py:1099
  18.4 4.2 %collective-permute-start.1 = (f32[13,16,128]{2,1,0:T(8,128)S(1)}, f32[13,16,128]{2,1,0:T(8,128)S(1)}, u32[]{:S(2)}, u32[]{:S(2)}) collective-permute-start(f32[13,16,128]{2,1,0:T(8,128)S(1)} %get-tuple-element.69), channel_id=1, source_target_pairs={{0,12},{1,13},{2,14},{3,15},{4,5},{5,4},{6,7},{7,6},{8,9},{9,8},{1... | collective-permute-start | bytes 319496 | tf_op jit(solution)/shard_map/cond/branch_0_fun/ppermute | solution.py:1012
  22.6 0.2 collective-permute-start
  22.7 0.5 %collective-permute-start.2 = (f32[16,128]{1,0:T(8,128)S(1)}, f32[16,128]{1,0:T(8,128)S(1)}, u32[]{:S(2)}, u32[]{:S(2)}) collective-permute-start(f32[16,128]{1,0:T(8,128)S(1)} %get-tuple-element.72), channel_id=1, source_target_pairs={{0,4},{1,5},{2,6},{3,7},{4,0},{5,1},{6,2},{7,3},{8,9},{9,8},{10,11... | collective-permute-start | bytes 24584 | tf_op jit(solution)/shard_map/cond/branch_0_fun/ppermute | solution.py:1012
  23.2 3.2 %collective-permute-done.2.beside_ref = f32[16,128]{1,0:T(8,128)S(1)} collective-permute-done((f32[16,128]{1,0:T(8,128)S(1)}, f32[16,128]{1,0:T(8,128)S(1)}, u32[]{:S(2)}, u32[]{:S(2)}) %collective-permute-start.2) | collective-permute-done | bytes 8224 | tf_op jit(solution)/shard_map/cond/branch_0_fun/ppermute | solution.py:1012
  26.4 0.5 %branch_0_fun.3.blend_ref = f32[9,16,128]{2,1,0:T(8,128)S(1)} custom-call(s32[2]{0:T(128)S(4)} %get-tuple-element.62.west_ref, f32[16]{0:T(128)S(4)} %get-tuple-element.71.weight_ref, f32[3,384,128]{2,1,0:T(8,128)S(1)} %get-tuple-element.64.field_ref, f32[11,16,128]{2,1,0:T(8,128)S(1)} %get-tuple-element.68.window_ref, ...), custom_call_target="tpu_custom_call" | custom-call | bytes 1138760 | tf_op jit(solution)/shard_map/cond/branch_0_fun/pallas_call | solution.py:952
  26.9 1.6 %collective-permute-start.3 = (f32[9,16,128]{2,1,0:T(8,128)S(1)}, f32[9,16,128]{2,1,0:T(8,128)S(1)}, u32[]{:S(2)}, u32[]{:S(2)}) collective-permute-start(f32[9,16,128]{2,1,0:T(8,128)S(1)} %branch_0_fun.3.blend_ref), channel_id=1, source_target_pairs={{0,2},{2,0},{1,3},{3,1},{4,6},{6,4},{5,7},{7,5},{8,10},{10,8},{9,1... | collective-permute-start | bytes 221192 | tf_op jit(solution)/shard_map/cond/branch_0_fun/ppermute | solution.py:1078
  28.7 2.7 %collective-permute-done.3.rows_ref = f32[9,16,128]{2,1,0:T(8,128)S(1)} collective-permute-done((f32[9,16,128]{2,1,0:T(8,128)S(1)}, f32[9,16,128]{2,1,0:T(8,128)S(1)}, u32[]{:S(2)}, u32[]{:S(2)}) %collective-permute-start.3) | collective-permute-done | bytes 73760 | tf_op jit(solution)/shard_map/cond/branch_0_fun/ppermute | solution.py:1078
  31.4 1.0 %branch_0_fun.5 = (f32[384,384]{1,0:T(8,128)}, f32[3,384,128]{2,1,0:T(8,128)S(1)}) custom-call(s32[2]{0:T(128)S(4)} %get-tuple-element.62.west_ref, s32[2]{0:T(128)S(4)} %get-tuple-element.63.south_ref, f32[3,384,128]{2,1,0:T(8,128)S(1)} %branch_0_fun.4.given_ref, f32[6,16,128]{2,1,0:T(8,128)S(1)} %get-tuple-element.75.speeds_ref, ...), custom_call_target="tpu_custom_call", output_to_operand_aliasing={{1}: (2, {})} | custom-call | bytes 1966096 | tf_op jit(solution)/shard_map/cond/branch_0_fun/pallas_call | solution.py:952
  (21 shorter events, 0.7 us)
Async XLA Ops:
  0.0 4.5 %copy-start.1 = (f32[16,24,384]{2,1,0:T(8,128)S(1)}, f32[16,24,384]{2,1,0:T(8,128)}, u32[]{:S(2)}) copy-start(f32[16,24,384]{2,1,0:T(8,128)} %param.9) | copy-start | bytes 1769476
  0.0 4.5 %copy-start.2 = (f32[16,24,384]{2,1,0:T(8,128)S(1)}, f32[16,24,384]{2,1,0:T(8,128)}, u32[]{:S(2)}) copy-start(f32[16,24,384]{2,1,0:T(8,128)} %param.10) | copy-start | bytes 1769476
  1.5 6.1 %collective-permute-start.8 = (f32[14,16,128]{2,1,0:T(8,128)S(1)}, f32[14,16,128]{2,1,0:T(8,128)S(1)}, u32[]{:S(2)}, u32[]{:S(2)}) collective-permute-start(f32[14,16,128]{2,1,0:T(8,128)S(1)} %get-tuple-element.110), channel_id=1, source_target_pairs={{0,2},{2,0},{1,3},{3,1},{4,6},{6,4},{5,7},{7,5},{8,10},{10,8},{9,1... | collective-permute-start | bytes 344072 | tf_op jit(solution)/shard_map/ppermute | solution.py:1002
  4.5 7.6 %copy-start = (f32[16,24,384]{2,1,0:T(8,128)S(1)}, f32[16,24,384]{2,1,0:T(8,128)}, u32[]{:S(2)}) copy-start(f32[16,24,384]{2,1,0:T(8,128)} %param.8) | copy-start | bytes 1769476
  4.8 0.7 %copy-start.3 = (s32[2]{0:T(128)S(1)}, s32[2]{0:T(128)}, u32[]{:S(2)}) copy-start(s32[2]{0:T(128)} %west_hbm.1) | copy-start | bytes 28
  4.9 7.9 %collective-permute-start.9 = (f32[12,16,128]{2,1,0:T(8,128)S(1)}, f32[12,16,128]{2,1,0:T(8,128)S(1)}, u32[]{:S(2)}, u32[]{:S(2)}) collective-permute-start(f32[12,16,128]{2,1,0:T(8,128)S(1)} %get-tuple-element.115), channel_id=1, source_target_pairs={{0,1},{1,0},{2,3},{3,2},{4,8},{5,9},{6,10},{7,11},{8,4},{9,5},{10,... | collective-permute-start | bytes 294920 | tf_op jit(solution)/shard_map/ppermute | solution.py:1012
  7.7 5.1 %collective-permute-start.10 = (f32[11,16,128]{2,1,0:T(8,128)S(1)}, f32[11,16,128]{2,1,0:T(8,128)S(1)}, u32[]{:S(2)}, u32[]{:S(2)}) collective-permute-start(f32[11,16,128]{2,1,0:T(8,128)S(1)} %slice_add_fusion), channel_id=1, source_target_pairs={{0,4},{1,5},{2,6},{3,7},{4,0},{5,1},{6,2},{7,3},{8,12},{9,13},{10,... | collective-permute-start | bytes 270344 | tf_op jit(solution)/shard_map/ppermute | solution.py:1012
  9.6 2.6 %collective-permute-start.11 = (f32[24,384]{1,0:T(8,128)S(1)}, f32[24,384]{1,0:T(8,128)S(1)}, u32[]{:S(2)}, u32[]{:S(2)}) collective-permute-start(f32[24,384]{1,0:T(8,128)S(1)} %get-tuple-element.118), channel_id=1, source_target_pairs={{0,1},{1,0},{2,3},{3,2},{4,5},{5,4},{6,7},{7,6},{8,9},{9,8},{10,11... | collective-permute-start | bytes 110600 | tf_op jit(solution)/shard_map/ppermute | solution.py:1003
  9.6 5.7 %collective-permute-start.13 = (f32[11,16,128]{2,1,0:T(8,128)S(1)}, f32[11,16,128]{2,1,0:T(8,128)S(1)}, u32[]{:S(2)}, u32[]{:S(2)}) collective-permute-start(f32[11,16,128]{2,1,0:T(8,128)S(1)} %slice_add_fusion), channel_id=1, source_target_pairs={{0,1},{1,0},{2,3},{3,2},{4,12},{5,13},{6,14},{7,15},{8,9},{9,8},{1... | collective-permute-start | bytes 270344 | tf_op jit(solution)/shard_map/ppermute | solution.py:1012
  10.1 5.5 %collective-permute-start.12 = (f32[11,16,128]{2,1,0:T(8,128)S(1)}, f32[11,16,128]{2,1,0:T(8,128)S(1)}, u32[]{:S(2)}, u32[]{:S(2)}) collective-permute-start(f32[11,16,128]{2,1,0:T(8,128)S(1)} %slice_add_fusion), channel_id=1, source_target_pairs={{0,12},{4,0},{8,4},{12,8},{1,13},{5,1},{9,5},{13,9},{2,14},{6,2},{... | collective-permute-start | bytes 270344 | tf_op jit(solution)/shard_map/ppermute | solution.py:1023
  13.4 4.7 %collective-permute-start.15 = (f32[11,16,128]{2,1,0:T(8,128)S(1)}, f32[11,16,128]{2,1,0:T(8,128)S(1)}, u32[]{:S(2)}, u32[]{:S(2)}) collective-permute-start(f32[11,16,128]{2,1,0:T(8,128)S(1)} %get-tuple-element.124), channel_id=1, source_target_pairs={{0,2},{2,0},{1,3},{3,1},{4,6},{6,4},{5,7},{7,5},{8,10},{10,8},{9,1... | collective-permute-start | bytes 270344 | tf_op jit(solution)/shard_map/ppermute | solution.py:1042
  15.8 1.3 %collective-permute-start.14 = (f32[24,384]{1,0:T(8,128)S(1)}, f32[24,384]{1,0:T(8,128)S(1)}, u32[]{:S(2)}, u32[]{:S(2)}) collective-permute-start(f32[24,384]{1,0:T(8,128)S(1)} %get-tuple-element.121), channel_id=1, source_target_pairs={{0,1},{1,0},{2,3},{3,2},{4,5},{5,4},{6,7},{7,6},{8,9},{9,8},{10,11... | collective-permute-start | bytes 110600 | tf_op jit(solution)/shard_map/ppermute | solution.py:1050
  18.4 8.1 %collective-permute-start.1 = (f32[13,16,128]{2,1,0:T(8,128)S(1)}, f32[13,16,128]{2,1,0:T(8,128)S(1)}, u32[]{:S(2)}, u32[]{:S(2)}) collective-permute-start(f32[13,16,128]{2,1,0:T(8,128)S(1)} %get-tuple-element.69), channel_id=1, source_target_pairs={{0,12},{1,13},{2,14},{3,15},{4,5},{5,4},{6,7},{7,6},{8,9},{9,8},{1... | collective-permute-start | bytes 319496 | tf_op jit(solution)/shard_map/cond/branch_0_fun/ppermute | solution.py:1012
  22.6 3.9 %collective-permute-start = (f32[11,16,128]{2,1,0:T(8,128)S(1)}, f32[11,16,128]{2,1,0:T(8,128)S(1)}, u32[]{:S(2)}, u32[]{:S(2)}) collective-permute-start(f32[11,16,128]{2,1,0:T(8,128)S(1)} %get-tuple-element.68.window_ref), channel_id=1, source_target_pairs={{0,1},{1,0},{2,3},{3,2},{4,12},{5,13},{6,14},{7,15},{8,9},{9,8},{1... | collective-permute-start | bytes 270344 | tf_op jit(solution)/shard_map/cond/branch_0_fun/ppermute | solution.py:1012
  22.7 3.7 %collective-permute-start.2 = (f32[16,128]{1,0:T(8,128)S(1)}, f32[16,128]{1,0:T(8,128)S(1)}, u32[]{:S(2)}, u32[]{:S(2)}) collective-permute-start(f32[16,128]{1,0:T(8,128)S(1)} %get-tuple-element.72), channel_id=1, source_target_pairs={{0,4},{1,5},{2,6},{3,7},{4,0},{5,1},{6,2},{7,3},{8,9},{9,8},{10,11... | collective-permute-start | bytes 24584 | tf_op jit(solution)/shard_map/cond/branch_0_fun/ppermute | solution.py:1012
  26.9 4.4 %collective-permute-start.3 = (f32[9,16,128]{2,1,0:T(8,128)S(1)}, f32[9,16,128]{2,1,0:T(8,128)S(1)}, u32[]{:S(2)}, u32[]{:S(2)}) collective-permute-start(f32[9,16,128]{2,1,0:T(8,128)S(1)} %branch_0_fun.3.blend_ref), channel_id=1, source_target_pairs={{0,2},{2,0},{1,3},{3,1},{4,6},{6,4},{5,7},{7,5},{8,10},{10,8},{9,1... | collective-permute-start | bytes 221192 | tf_op jit(solution)/shard_map/cond/branch_0_fun/ppermute | solution.py:1078

commit v3 on v2

--- a/solution.py
+++ b/solution.py
@@ -629,8 +629,8 @@
     east_ref,
     speeds_ref,
     three_ref,
+    one_ref,
     two_ref,
-    one_ref,
     field_ref,
     edge_ref,
     own_ref,
@@ -1043,7 +1043,7 @@
     first, edge, own = call(
         kernel(first_kernel),
         [chunked, (height, breadth), slabs(slots + 1)],
-        [west, south, early, east, speeds, *starting[::-1]],
+        [west, south, early, east, speeds, starting[2], starting[0], starting[1]],
         "ssvvvvvv",
         flops=10 * size * breadth,
     )

time: 32.5 us -> 31.6 us (0.972)
  the two profiles are of different devices: /device:TPU:0 before, /device:TPU:14 now
where the time goes in v3:
time: 31.6 us
  waiting for transfers between devices  13.8 us (44%)
  starting transfers between devices  11.2 us (35%)
  Pallas kernels  5.18 us (16%)
  between operations  0.74 us (2%)
  local copies, waits for them, and re-layouts  0.6 us (2%)
    ppermute x6, starting transfers between devices, over_tiles(): return lax.ppermute(message, ('tiles', 'rows', 'lev'), pairs)  9.34 us
    ppermute x6, waiting for transfers between devices, over_tiles(): return lax.ppermute(message, ('tiles', 'rows', 'lev'), pairs)  7.38 us
    pallas_call x10, Pallas kernels, call(): pl.pallas_call(kernel, out_shape=outs, in_specs=[pl.BlockSpec(memory_spac...  5.18 us
    ppermute x1, waiting for transfers between devices, finish(): rows = lax.ppermute(blend, 'rows', swap)  3.6 us
    ppermute x1, waiting for transfers between devices, per_device_paired(): level = lax.ppermute(edge, 'lev', swap)  1.18 us
    ppermute x1, waiting for transfers between devices, per_device_paired(): rows = lax.ppermute(rows, 'rows', swap)  1.15 us
  transfers between devices with their start and end apart: 12, of which 8 were waited for; matrix products, arithmetic and copies ran while one was open for 2% of the time, Pallas kernels for 6%

profile of v3, /device:TPU:14, one launch (start us, length us, event | category | flops | bytes accessed | tf_op | source)
XLA Modules:
  0.0 31.6 jit_solution(15989855165306215622)
XLA Ops:
  0.0 1.5 %shard_map.66 = (f32[14,16,128]{2,1,0:T(8,128)S(1)}, f32[3,384,128]{2,1,0:T(8,128)S(1)}, s32[2]{0:T(128)S(4)}, s32[2]{0:T(128)S(4)}, f32[16]{0:T(128)S(4)}) custom-call(s32[2]{0:T(128)} %west_hbm.1, s32[2]{0:T(128)} %south_hbm.1, f32[16]{0:T(128)} %weight_hbm.1, f32[384,384]{1,0:T(8,128)} %bitcast.6, f32[384,384]{1,0:T(8,128)} %bitcast.15), custom_call_target="tpu_custom_call" | custom-call | bytes 1884320 | tf_op jit(solution)/shard_map/pallas_call | solution.py:952
  1.5 0.6 %collective-permute-start.8 = (f32[14,16,128]{2,1,0:T(8,128)S(1)}, f32[14,16,128]{2,1,0:T(8,128)S(1)}, u32[]{:S(2)}, u32[]{:S(2)}) collective-permute-start(f32[14,16,128]{2,1,0:T(8,128)S(1)} %get-tuple-element.110), channel_id=1, source_target_pairs={{0,2},{2,0},{1,3},{3,1},{4,6},{6,4},{5,7},{7,5},{8,10},{10,8},{9,1... | collective-permute-start | bytes 344072 | tf_op jit(solution)/shard_map/ppermute | solution.py:1002
  2.1 0.3 shard_map.67
  2.5 1.6 %collective-permute-start.9 = (f32[12,16,128]{2,1,0:T(8,128)S(1)}, f32[12,16,128]{2,1,0:T(8,128)S(1)}, u32[]{:S(2)}, u32[]{:S(2)}) collective-permute-start(f32[12,16,128]{2,1,0:T(8,128)S(1)} %get-tuple-element.115), channel_id=1, source_target_pairs={{0,1},{1,0},{2,3},{3,2},{4,8},{5,9},{6,10},{7,11},{8,4},{9,5},{10,... | collective-permute-start | bytes 294920 | tf_op jit(solution)/shard_map/ppermute | solution.py:1012
  4.1 0.6 %slice.6 = s32[1]{0:T(128)} slice(s32[2]{0:T(128)S(1)} %copy-done.3), slice={[1:2]} | slice | bytes 8 | tf_op jit(solution)/shard_map/slice | solution.py:1015
  5.3 1.1 %collective-permute-done.8.rows_ref = f32[14,16,128]{2,1,0:T(8,128)S(1)} collective-permute-done((f32[14,16,128]{2,1,0:T(8,128)S(1)}, f32[14,16,128]{2,1,0:T(8,128)S(1)}, u32[]{:S(2)}, u32[]{:S(2)}) %collective-permute-start.8) | collective-permute-done | bytes 114720 | tf_op jit(solution)/shard_map/ppermute | solution.py:1002
  6.5 0.5 %collective-permute-start.10 = (f32[11,16,128]{2,1,0:T(8,128)S(1)}, f32[11,16,128]{2,1,0:T(8,128)S(1)}, u32[]{:S(2)}, u32[]{:S(2)}) collective-permute-start(f32[11,16,128]{2,1,0:T(8,128)S(1)} %slice_add_fusion), channel_id=1, source_target_pairs={{0,4},{1,5},{2,6},{3,7},{4,0},{5,1},{6,2},{7,3},{8,12},{9,13},{10,... | collective-permute-start | bytes 270344 | tf_op jit(solution)/shard_map/ppermute | solution.py:1012
  7.0 2.6 %collective-permute-start.13 = (f32[11,16,128]{2,1,0:T(8,128)S(1)}, f32[11,16,128]{2,1,0:T(8,128)S(1)}, u32[]{:S(2)}, u32[]{:S(2)}) collective-permute-start(f32[11,16,128]{2,1,0:T(8,128)S(1)} %slice_add_fusion), channel_id=1, source_target_pairs={{0,1},{1,0},{2,3},{3,2},{4,12},{5,13},{6,14},{7,15},{8,9},{9,8},{1... | collective-permute-start | bytes 270344 | tf_op jit(solution)/shard_map/ppermute | solution.py:1012
  9.6 0.6 %shard_map.68.given_ref = f32[3,384,128]{2,1,0:T(8,128)S(1)} custom-call(f32[384,384]{1,0:T(8,128)S(1)} %bitcast.7, f32[384,384]{1,0:T(8,128)S(1)} %bitcast.9, f32[384,384]{1,0:T(8,128)S(1)} %bitcast.17, f32[14,16,128]{2,1,0:T(8,128)S(1)} %collective-permute-done.8.rows_ref, f32[24,384]{1,0:T(8,128)S(1)} %collective-permute-done.11.level_ref), custom_call_target="tpu_custom_call" | custom-call | flops 4423680 | bytes 2510848 | tf_op jit(solution)/shard_map/pallas_call | solution.py:952
  10.2 0.8 %collective-permute-done.10.one_ref = f32[11,16,128]{2,1,0:T(8,128)S(1)} collective-permute-done((f32[11,16,128]{2,1,0:T(8,128)S(1)}, f32[11,16,128]{2,1,0:T(8,128)S(1)}, u32[]{:S(2)}, u32[]{:S(2)}) %collective-permute-start.10) | collective-permute-done | bytes 90144 | tf_op jit(solution)/shard_map/ppermute | solution.py:1012
  11.1 0.6 %shard_map.69 = (f32[3,384,128]{2,1,0:T(8,128)S(1)}, f32[11,16,128]{2,1,0:T(8,128)S(1)}) custom-call(s32[2]{0:T(128)S(4)} %get-tuple-element.112.west_ref, s32[2]{0:T(128)S(4)} %get-tuple-element.113.south_ref, f32[384,384]{1,0:T(8,128)S(1)} %bitcast.10, f32[12,16,128]{2,1,0:T(8,128)S(1)} %collective-permute-done.9.three_ref, ...), custom_call_target="tpu_custom_call", output_to_operand_aliasing={{0}: (5, {})} | custom-call | flops 1474560 | bytes 2048016 | tf_op jit(solution)/shard_map/pallas_call | solution.py:952
  11.7 0.6 %collective-permute-start.15 = (f32[11,16,128]{2,1,0:T(8,128)S(1)}, f32[11,16,128]{2,1,0:T(8,128)S(1)}, u32[]{:S(2)}, u32[]{:S(2)}) collective-permute-start(f32[11,16,128]{2,1,0:T(8,128)S(1)} %get-tuple-element.124), channel_id=1, source_target_pairs={{0,2},{2,0},{1,3},{3,1},{4,6},{6,4},{5,7},{7,5},{8,10},{10,8},{9,1... | collective-permute-start | bytes 270344 | tf_op jit(solution)/shard_map/ppermute | solution.py:1042
  12.3 2.6 %collective-permute-done.13.two_ref = f32[11,16,128]{2,1,0:T(8,128)S(1)} collective-permute-done((f32[11,16,128]{2,1,0:T(8,128)S(1)}, f32[11,16,128]{2,1,0:T(8,128)S(1)}, u32[]{:S(2)}, u32[]{:S(2)}) %collective-permute-start.13) | collective-permute-done | bytes 90144 | tf_op jit(solution)/shard_map/ppermute | solution.py:1012
  15.0 0.5 %collective-permute-done.12.three_ref = f32[11,16,128]{2,1,0:T(8,128)S(1)} collective-permute-done((f32[11,16,128]{2,1,0:T(8,128)S(1)}, f32[11,16,128]{2,1,0:T(8,128)S(1)}, u32[]{:S(2)}, u32[]{:S(2)}) %collective-permute-start.12) | collective-permute-done | bytes 90144 | tf_op jit(solution)/shard_map/ppermute | solution.py:1023
  15.8 1.2 %collective-permute-done.14.level_ref = f32[24,384]{1,0:T(8,128)S(1)} collective-permute-done((f32[24,384]{1,0:T(8,128)S(1)}, f32[24,384]{1,0:T(8,128)S(1)}, u32[]{:S(2)}, u32[]{:S(2)}) %collective-permute-start.14) | collective-permute-done | bytes 36896 | tf_op jit(solution)/shard_map/ppermute | solution.py:1050
  17.1 14.5 %conditional.1 = (f32[16,24,384]{2,1,0:T(8,128)}) conditional(s32[]{:T(128)} %convert_element_type.3, (f32[11,16,128]{2,1,0:T(8,128)S(1)}, f32[13,16,128]{2,1,0:T(8,128)S(1)}, f32[16,128]{1,0:T(8,128)S(1)}, s32[2]{0:T(128)S(4)}, f32[16]{0:T(128)S(4)}, /*index=5*/f32[3,384,128]{2,1,0:T(8,128)S(1)}, f32[11,16,128]{2,1,0:T(8,128)S(1)}, ...), branch_computations={%region_0.0_spmd, %region_1.0_spmd} | conditional | flops 4423680 | bytes 7475472 | solution.py:1099
  17.4 2.8 %collective-permute-start = (f32[11,16,128]{2,1,0:T(8,128)S(1)}, f32[11,16,128]{2,1,0:T(8,128)S(1)}, u32[]{:S(2)}, u32[]{:S(2)}) collective-permute-start(f32[11,16,128]{2,1,0:T(8,128)S(1)} %get-tuple-element.68.window_ref), channel_id=1, source_target_pairs={{0,1},{1,0},{2,3},{3,2},{4,12},{5,13},{6,14},{7,15},{8,9},{9,8},{1... | collective-permute-start | bytes 270344 | tf_op jit(solution)/shard_map/cond/branch_0_fun/ppermute | solution.py:1012
  20.2 1.6 %collective-permute-start.2 = (f32[16,128]{1,0:T(8,128)S(1)}, f32[16,128]{1,0:T(8,128)S(1)}, u32[]{:S(2)}, u32[]{:S(2)}) collective-permute-start(f32[16,128]{1,0:T(8,128)S(1)} %get-tuple-element.72), channel_id=1, source_target_pairs={{0,4},{1,5},{2,6},{3,7},{4,0},{5,1},{6,2},{7,3},{8,9},{9,8},{10,11... | collective-permute-start | bytes 24584 | tf_op jit(solution)/shard_map/cond/branch_0_fun/ppermute | solution.py:1012
  21.8 3.4 %collective-permute-done.2.beside_ref = f32[16,128]{1,0:T(8,128)S(1)} collective-permute-done((f32[16,128]{1,0:T(8,128)S(1)}, f32[16,128]{1,0:T(8,128)S(1)}, u32[]{:S(2)}, u32[]{:S(2)}) %collective-permute-start.2) | collective-permute-done | bytes 8224 | tf_op jit(solution)/shard_map/cond/branch_0_fun/ppermute | solution.py:1012
  25.1 0.5 %collective-permute-done.middle_ref = f32[11,16,128]{2,1,0:T(8,128)S(1)} collective-permute-done((f32[11,16,128]{2,1,0:T(8,128)S(1)}, f32[11,16,128]{2,1,0:T(8,128)S(1)}, u32[]{:S(2)}, u32[]{:S(2)}) %collective-permute-start) | collective-permute-done | bytes 90144 | tf_op jit(solution)/shard_map/cond/branch_0_fun/ppermute | solution.py:1012
  25.6 0.5 %branch_0_fun.3.blend_ref = f32[9,16,128]{2,1,0:T(8,128)S(1)} custom-call(s32[2]{0:T(128)S(4)} %get-tuple-element.62.west_ref, f32[16]{0:T(128)S(4)} %get-tuple-element.71.weight_ref, f32[3,384,128]{2,1,0:T(8,128)S(1)} %get-tuple-element.64.field_ref, f32[11,16,128]{2,1,0:T(8,128)S(1)} %get-tuple-element.68.window_ref, ...), custom_call_target="tpu_custom_call" | custom-call | bytes 1138760 | tf_op jit(solution)/shard_map/cond/branch_0_fun/pallas_call | solution.py:952
  26.1 0.6 %collective-permute-start.3 = (f32[9,16,128]{2,1,0:T(8,128)S(1)}, f32[9,16,128]{2,1,0:T(8,128)S(1)}, u32[]{:S(2)}, u32[]{:S(2)}) collective-permute-start(f32[9,16,128]{2,1,0:T(8,128)S(1)} %branch_0_fun.3.blend_ref), channel_id=1, source_target_pairs={{0,2},{2,0},{1,3},{3,1},{4,6},{6,4},{5,7},{7,5},{8,10},{10,8},{9,1... | collective-permute-start | bytes 221192 | tf_op jit(solution)/shard_map/cond/branch_0_fun/ppermute | solution.py:1078
  27.0 3.6 %collective-permute-done.3.rows_ref = f32[9,16,128]{2,1,0:T(8,128)S(1)} collective-permute-done((f32[9,16,128]{2,1,0:T(8,128)S(1)}, f32[9,16,128]{2,1,0:T(8,128)S(1)}, u32[]{:S(2)}, u32[]{:S(2)}) %collective-permute-start.3) | collective-permute-done | bytes 73760 | tf_op jit(solution)/shard_map/cond/branch_0_fun/ppermute | solution.py:1078
  30.6 1.1 %branch_0_fun.5 = (f32[384,384]{1,0:T(8,128)}, f32[3,384,128]{2,1,0:T(8,128)S(1)}) custom-call(s32[2]{0:T(128)S(4)} %get-tuple-element.62.west_ref, s32[2]{0:T(128)S(4)} %get-tuple-element.63.south_ref, f32[3,384,128]{2,1,0:T(8,128)S(1)} %branch_0_fun.4.given_ref, f32[6,16,128]{2,1,0:T(8,128)S(1)} %get-tuple-element.75.speeds_ref, ...), custom_call_target="tpu_custom_call", output_to_operand_aliasing={{1}: (2, {})} | custom-call | bytes 1966096 | tf_op jit(solution)/shard_map/cond/branch_0_fun/pallas_call | solution.py:952
  (21 shorter events, 0.9 us)
Async XLA Ops:
  0.0 2.1 %copy-start.1 = (f32[16,24,384]{2,1,0:T(8,128)S(1)}, f32[16,24,384]{2,1,0:T(8,128)}, u32[]{:S(2)}) copy-start(f32[16,24,384]{2,1,0:T(8,128)} %param.9) | copy-start | bytes 1769476
  0.0 2.1 %copy-start.2 = (f32[16,24,384]{2,1,0:T(8,128)S(1)}, f32[16,24,384]{2,1,0:T(8,128)}, u32[]{:S(2)}) copy-start(f32[16,24,384]{2,1,0:T(8,128)} %param.10) | copy-start | bytes 1769476
  1.5 5.0 %collective-permute-start.8 = (f32[14,16,128]{2,1,0:T(8,128)S(1)}, f32[14,16,128]{2,1,0:T(8,128)S(1)}, u32[]{:S(2)}, u32[]{:S(2)}) collective-permute-start(f32[14,16,128]{2,1,0:T(8,128)S(1)} %get-tuple-element.110), channel_id=1, source_target_pairs={{0,2},{2,0},{1,3},{3,1},{4,6},{6,4},{5,7},{7,5},{8,10},{10,8},{9,1... | collective-permute-start | bytes 344072 | tf_op jit(solution)/shard_map/ppermute | solution.py:1002
  2.1 7.5 %copy-start = (f32[16,24,384]{2,1,0:T(8,128)S(1)}, f32[16,24,384]{2,1,0:T(8,128)}, u32[]{:S(2)}) copy-start(f32[16,24,384]{2,1,0:T(8,128)} %param.8) | copy-start | bytes 1769476
  2.4 1.7 %copy-start.3 = (s32[2]{0:T(128)S(1)}, s32[2]{0:T(128)}, u32[]{:S(2)}) copy-start(s32[2]{0:T(128)} %west_hbm.1) | copy-start | bytes 28
  2.5 7.8 %collective-permute-start.9 = (f32[12,16,128]{2,1,0:T(8,128)S(1)}, f32[12,16,128]{2,1,0:T(8,128)S(1)}, u32[]{:S(2)}, u32[]{:S(2)}) collective-permute-start(f32[12,16,128]{2,1,0:T(8,128)S(1)} %get-tuple-element.115), channel_id=1, source_target_pairs={{0,1},{1,0},{2,3},{3,2},{4,8},{5,9},{6,10},{7,11},{8,4},{9,5},{10,... | collective-permute-start | bytes 294920 | tf_op jit(solution)/shard_map/ppermute | solution.py:1012
  6.5 4.6 %collective-permute-start.10 = (f32[11,16,128]{2,1,0:T(8,128)S(1)}, f32[11,16,128]{2,1,0:T(8,128)S(1)}, u32[]{:S(2)}, u32[]{:S(2)}) collective-permute-start(f32[11,16,128]{2,1,0:T(8,128)S(1)} %slice_add_fusion), channel_id=1, source_target_pairs={{0,4},{1,5},{2,6},{3,7},{4,0},{5,1},{6,2},{7,3},{8,12},{9,13},{10,... | collective-permute-start | bytes 270344 | tf_op jit(solution)/shard_map/ppermute | solution.py:1012
  7.0 2.6 %collective-permute-start.11 = (f32[24,384]{1,0:T(8,128)S(1)}, f32[24,384]{1,0:T(8,128)S(1)}, u32[]{:S(2)}, u32[]{:S(2)}) collective-permute-start(f32[24,384]{1,0:T(8,128)S(1)} %get-tuple-element.118), channel_id=1, source_target_pairs={{0,1},{1,0},{2,3},{3,2},{4,5},{5,4},{6,7},{7,6},{8,9},{9,8},{10,11... | collective-permute-start | bytes 110600 | tf_op jit(solution)/shard_map/ppermute | solution.py:1003
  7.0 8.0 %collective-permute-start.13 = (f32[11,16,128]{2,1,0:T(8,128)S(1)}, f32[11,16,128]{2,1,0:T(8,128)S(1)}, u32[]{:S(2)}, u32[]{:S(2)}) collective-permute-start(f32[11,16,128]{2,1,0:T(8,128)S(1)} %slice_add_fusion), channel_id=1, source_target_pairs={{0,1},{1,0},{2,3},{3,2},{4,12},{5,13},{6,14},{7,15},{8,9},{9,8},{1... | collective-permute-start | bytes 270344 | tf_op jit(solution)/shard_map/ppermute | solution.py:1012
  9.6 5.9 %collective-permute-start.12 = (f32[11,16,128]{2,1,0:T(8,128)S(1)}, f32[11,16,128]{2,1,0:T(8,128)S(1)}, u32[]{:S(2)}, u32[]{:S(2)}) collective-permute-start(f32[11,16,128]{2,1,0:T(8,128)S(1)} %slice_add_fusion), channel_id=1, source_target_pairs={{0,12},{4,0},{8,4},{12,8},{1,13},{5,1},{9,5},{13,9},{2,14},{6,2},{... | collective-permute-start | bytes 270344 | tf_op jit(solution)/shard_map/ppermute | solution.py:1023
  11.7 5.2 %collective-permute-start.15 = (f32[11,16,128]{2,1,0:T(8,128)S(1)}, f32[11,16,128]{2,1,0:T(8,128)S(1)}, u32[]{:S(2)}, u32[]{:S(2)}) collective-permute-start(f32[11,16,128]{2,1,0:T(8,128)S(1)} %get-tuple-element.124), channel_id=1, source_target_pairs={{0,2},{2,0},{1,3},{3,1},{4,6},{6,4},{5,7},{7,5},{8,10},{10,8},{9,1... | collective-permute-start | bytes 270344 | tf_op jit(solution)/shard_map/ppermute | solution.py:1042
  15.7 1.3 %collective-permute-start.14 = (f32[24,384]{1,0:T(8,128)S(1)}, f32[24,384]{1,0:T(8,128)S(1)}, u32[]{:S(2)}, u32[]{:S(2)}) collective-permute-start(f32[24,384]{1,0:T(8,128)S(1)} %get-tuple-element.121), channel_id=1, source_target_pairs={{0,1},{1,0},{2,3},{3,2},{4,5},{5,4},{6,7},{7,6},{8,9},{9,8},{10,11... | collective-permute-start | bytes 110600 | tf_op jit(solution)/shard_map/ppermute | solution.py:1050
  17.1 8.5 %collective-permute-start.1 = (f32[13,16,128]{2,1,0:T(8,128)S(1)}, f32[13,16,128]{2,1,0:T(8,128)S(1)}, u32[]{:S(2)}, u32[]{:S(2)}) collective-permute-start(f32[13,16,128]{2,1,0:T(8,128)S(1)} %get-tuple-element.69), channel_id=1, source_target_pairs={{0,12},{1,13},{2,14},{3,15},{4,5},{5,4},{6,7},{7,6},{8,9},{9,8},{1... | collective-permute-start | bytes 319496 | tf_op jit(solution)/shard_map/cond/branch_0_fun/ppermute | solution.py:1012
  17.4 8.3 %collective-permute-start = (f32[11,16,128]{2,1,0:T(8,128)S(1)}, f32[11,16,128]{2,1,0:T(8,128)S(1)}, u32[]{:S(2)}, u32[]{:S(2)}) collective-permute-start(f32[11,16,128]{2,1,0:T(8,128)S(1)} %get-tuple-element.68.window_ref), channel_id=1, source_target_pairs={{0,1},{1,0},{2,3},{3,2},{4,12},{5,13},{6,14},{7,15},{8,9},{9,8},{1... | collective-permute-start | bytes 270344 | tf_op jit(solution)/shard_map/cond/branch_0_fun/ppermute | solution.py:1012
  20.2 4.9 %collective-permute-start.2 = (f32[16,128]{1,0:T(8,128)S(1)}, f32[16,128]{1,0:T(8,128)S(1)}, u32[]{:S(2)}, u32[]{:S(2)}) collective-permute-start(f32[16,128]{1,0:T(8,128)S(1)} %get-tuple-element.72), channel_id=1, source_target_pairs={{0,4},{1,5},{2,6},{3,7},{4,0},{5,1},{6,2},{7,3},{8,9},{9,8},{10,11... | collective-permute-start | bytes 24584 | tf_op jit(solution)/shard_map/cond/branch_0_fun/ppermute | solution.py:1012
  26.1 4.4 %collective-permute-start.3 = (f32[9,16,128]{2,1,0:T(8,128)S(1)}, f32[9,16,128]{2,1,0:T(8,128)S(1)}, u32[]{:S(2)}, u32[]{:S(2)}) collective-permute-start(f32[9,16,128]{2,1,0:T(8,128)S(1)} %branch_0_fun.3.blend_ref), channel_id=1, source_target_pairs={{0,2},{2,0},{1,3},{3,1},{4,6},{6,4},{5,7},{7,5},{8,10},{10,8},{9,1... | collective-permute-start | bytes 221192 | tf_op jit(solution)/shard_map/cond/branch_0_fun/ppermute | solution.py:1078
